TPU v7x, 512 devices: a whole 4x8x8 slice. The times are simulated.
512 devices in a mesh: replica: 8 (over z), fsdp: 8 (over x, core), tensor: 8 (over y).
Axes of the slice: x: 4, y: 8, z: 8, core: 2. Of those that a mesh axis runs over, the one named last changes fastest.
Arguments:
- momentum: bfloat16 [8, 4096, 14336], P('replica', 'fsdp', 'tensor'), may hold values from -64 to 64
- q_prev: bfloat16 [14336, 128], P('tensor'), may hold values from -4 to 4
Outputs:
- momentum_next: bfloat16 [8, 4096, 14336], P('replica', 'fsdp', 'tensor')
- update_left: float32 [4096, 128], P('fsdp')
- q_next: bfloat16 [14336, 128], P('tensor')
All inputs are finite; a program needn't handle non-finite values.
Results may differ from a plain program's by a relative error of at most 0.02.
Values may be sent and summed in bfloat16 or wider, within the bound.
A program may use at most 64 MiB of HBM per device.

v0:
```python
import math

import jax
import jax.numpy as jnp
from jax import lax
from jax.sharding import PartitionSpec as P

D = 4096
FF = 14336
ITERS = 3


ridge_scale = 1e-06
norm_eps = 1e-06
momentum_decay = 0.95


def orthonormal(rows, gram_total):
    rank = gram_total.shape[0]
    ridge = ridge_scale * jnp.trace(gram_total) / rank
    lower_factor = jnp.linalg.cholesky(gram_total + ridge * jnp.eye(rank, dtype=jnp.float32))
    return lax.linalg.triangular_solve(
        lower_factor, rows, left_side=False, lower=True, transpose_a=True
    )


def gram_of(rows):
    return jnp.einsum("dr,ds->rs", rows, rows, precision=lax.Precision.HIGHEST)


def column_scale(right_rows, column_sq):
    return (math.sqrt(FF) * right_rows / jnp.sqrt(column_sq + norm_eps)).astype(jnp.bfloat16)


def shards(momentum, q_prev):
    local_block = momentum[0]
    replicas = lax.axis_size("replica")
    factor_round = q_prev
    for iteration in range(ITERS):
        left_partial = jnp.dot(local_block, factor_round, preferred_element_type=jnp.float32)
        left_total = lax.psum(left_partial, ("replica", "tensor")) / replicas
        gram_total = lax.psum(gram_of(left_total).astype(jnp.bfloat16), "fsdp").astype(jnp.float32)
        left_round = orthonormal(left_total, gram_total).astype(jnp.bfloat16)
        right_partial = jnp.einsum(
            "dc,dr->cr", local_block, left_round, preferred_element_type=jnp.float32
        )
        right_total = lax.psum(right_partial, ("replica", "fsdp")) / replicas
        column_sq = lax.psum(jnp.sum(right_total * right_total, axis=0), "tensor")
        factor_round = column_scale(right_total, column_sq)
    right_round = right_total.astype(jnp.bfloat16)
    correction = jnp.einsum(
        "dr,cr->dc", left_round, right_round, preferred_element_type=jnp.float32
    )
    momentum_next = (local_block.astype(jnp.float32) - (1.0 - momentum_decay) * correction).astype(
        jnp.bfloat16
    )[None]
    update_left = math.sqrt(D) * left_round.astype(jnp.float32)
    return (momentum_next, update_left, factor_round)


def solution(mesh):
    in_specs = (P("replica", "fsdp", "tensor"), P("tensor", None))
    out_specs = (P("replica", "fsdp", "tensor"), P("fsdp", None), P("tensor", None))
    return jax.shard_map(shards, mesh=mesh, in_specs=in_specs, out_specs=out_specs, check_vma=False)
```

profile of v0, /device:TPU:1, one launch (start us, length us, event | category | flops | bytes accessed | tf_op | source)
XLA Modules:
  0.0 1263.9 jit_solution(17250489376571601639)
XLA Ops:
  8.2 2.8 fusion.8
  11.1 154.1 %all-reduce.7.cloned.1.call-done = f32[512,128]{1,0:T(8,128)} async-done(((f32[512,128]{1,0:T(8,128)}), f32[512,128]{1,0:T(8,128)}) %all-reduce.7.cloned.1.call-update) | async-done | bytes 262160 | tf_op jit(solution)/shard_map/psum | solution.py:41
  165.2 1.6 convolution_convert_fusion.2
  166.9 24.8 %psum.85 = bf16[128,128]{0,1:T(8,128)(2,1)S(1)} all-reduce(bf16[128,128]{0,1:T(8,128)(2,1)S(1)} %convolution_convert_fusion.2), channel_id=1, replica_groups=mesh['replica'=8,'fsdp'=8,'tensor'=8] {'fsdp'}, use_global_device_ids=true, to_apply=%region_1.0 | all-reduce | flops 16384 | bytes 65536 | tf_op jit(solution)/shard_map/psum | solution.py:42
  193.1 11.7 cholesky.59
  206.1 9.8 custom-call.7
  216.0 1.4 fusion.16
  218.8 193.0 %all-reduce.9.cloned.1.call-done = f32[1792,128]{0,1:T(8,128)} async-done(((f32[1792,128]{0,1:T(8,128)}), f32[1792,128]{0,1:T(8,128)}) %all-reduce.9.cloned.1.call-update) | async-done | bytes 917520 | tf_op jit(solution)/shard_map/psum | solution.py:47
  413.1 13.4 %psum.87 = f32[128]{0:T(128)S(1)} all-reduce(f32[128]{0:T(128)S(1)} %multiply_reduce_fusion.2), channel_id=1, replica_groups=mesh['replica'=8,'fsdp'=8,'tensor'=8] {'tensor'}, use_global_device_ids=true, to_apply=%region_7.10 | all-reduce | flops 128 | bytes 1024 | tf_op jit(solution)/shard_map/psum | solution.py:48
  426.5 2.6 fusion.10
  429.2 148.2 %all-reduce.11.cloned.1.call-done = f32[512,128]{1,0:T(8,128)} async-done(((f32[512,128]{1,0:T(8,128)}), f32[512,128]{1,0:T(8,128)}) %all-reduce.11.cloned.1.call-update) | async-done | bytes 262160 | tf_op jit(solution)/shard_map/psum | solution.py:41
  577.4 1.6 convolution_convert_fusion.1
  579.1 25.0 %psum.89 = bf16[128,128]{0,1:T(8,128)(2,1)S(1)} all-reduce(bf16[128,128]{0,1:T(8,128)(2,1)S(1)} %convolution_convert_fusion.1), channel_id=1, replica_groups=mesh['replica'=8,'fsdp'=8,'tensor'=8] {'fsdp'}, use_global_device_ids=true, to_apply=%region_9.12 | all-reduce | flops 16384 | bytes 65536 | tf_op jit(solution)/shard_map/psum | solution.py:42
  605.5 11.7 cholesky.70
  618.5 9.8 custom-call.8
  628.3 1.4 fusion.17
  631.1 193.0 %all-reduce.13.cloned.1.call-done = f32[1792,128]{0,1:T(8,128)} async-done(((f32[1792,128]{0,1:T(8,128)}), f32[1792,128]{0,1:T(8,128)}) %all-reduce.13.cloned.1.call-update) | async-done | bytes 917520 | tf_op jit(solution)/shard_map/psum | solution.py:47
  824.1 1.4 multiply_reduce_fusion.1
  825.5 13.4 %psum.91 = f32[128]{0:T(128)S(1)} all-reduce(f32[128]{0:T(128)S(1)} %multiply_reduce_fusion.1), channel_id=1, replica_groups=mesh['replica'=8,'fsdp'=8,'tensor'=8] {'tensor'}, use_global_device_ids=true, to_apply=%region_13.16 | all-reduce | flops 128 | bytes 1024 | tf_op jit(solution)/shard_map/psum | solution.py:48
  838.9 2.6 fusion.13
  841.5 148.2 %all-reduce.15.cloned.1.call-done = f32[512,128]{1,0:T(8,128)} async-done(((f32[512,128]{1,0:T(8,128)}), f32[512,128]{1,0:T(8,128)}) %all-reduce.15.cloned.1.call-update) | async-done | bytes 262160 | tf_op jit(solution)/shard_map/psum | solution.py:41
  989.8 1.6 convolution_convert_fusion
  991.4 25.0 %psum.93 = bf16[128,128]{0,1:T(8,128)(2,1)S(1)} all-reduce(bf16[128,128]{0,1:T(8,128)(2,1)S(1)} %convolution_convert_fusion), channel_id=1, replica_groups=mesh['replica'=8,'fsdp'=8,'tensor'=8] {'fsdp'}, use_global_device_ids=true, to_apply=%region_15.18 | all-reduce | flops 16384 | bytes 65536 | tf_op jit(solution)/shard_map/psum | solution.py:42
  1017.9 11.7 cholesky.81
  1030.9 9.8 custom-call.9
  1040.7 1.4 convert_multiply_fusion
  1044.3 191.9 %all-reduce.17.cloned.1.call-done = f32[1792,128]{0,1:T(8,128)} async-done(((f32[1792,128]{0,1:T(8,128)}), f32[1792,128]{0,1:T(8,128)}) %all-reduce.17.cloned.1.call-update) | async-done | bytes 917520 | tf_op jit(solution)/shard_map/psum | solution.py:47
  1236.3 1.4 multiply_reduce_fusion
  1237.7 13.4 %psum.95 = f32[128]{0:T(128)S(1)} all-reduce(f32[128]{0:T(128)S(1)} %multiply_reduce_fusion), channel_id=1, replica_groups=mesh['replica'=8,'fsdp'=8,'tensor'=8] {'tensor'}, use_global_device_ids=true, to_apply=%region_19.22 | all-reduce | flops 128 | bytes 1024 | tf_op jit(solution)/shard_map/psum | solution.py:48
  1251.1 2.1 divide_convert_fusion
  1253.2 2.0 copy.14
  1255.2 1.9 fusion
  (47 shorter events, 13.8 us)
Async XLA Ops:
  7.2 1.0 copy-start
  7.2 210.2 %copy-start.1 = (bf16[1,512,1792]{2,1,0:T(8,128)(2,1)S(1)}, bf16[1,512,1792]{2,1,0:T(8,128)(2,1)}, u32[]{:S(2)}) copy-start(bf16[1,512,1792]{2,1,0:T(8,128)(2,1)} %param.5) | copy-start | bytes 5505028
  7.2 158.0 %all-reduce.7.cloned.1.call-start = ((), (), s32[]{:S(2)}) async-start(), calls=%async_computation | async-start | bytes 524288 | tf_op jit(solution)/shard_map/psum | solution.py:41
  11.1 400.7 %all-reduce.9.cloned.1.call-start = ((), (), s32[]{:S(2)}) async-start(), calls=%async_computation.1 | async-start | bytes 1835008 | tf_op jit(solution)/shard_map/psum | solution.py:47
  218.7 358.7 %all-reduce.11.cloned.1.call-start = ((), (), s32[]{:S(2)}) async-start(), calls=%async_computation.2 | async-start | bytes 524288 | tf_op jit(solution)/shard_map/psum | solution.py:41
  429.1 395.0 %all-reduce.13.cloned.1.call-start = ((), (), s32[]{:S(2)}) async-start(), calls=%async_computation.3 | async-start | bytes 1835008 | tf_op jit(solution)/shard_map/psum | solution.py:47
  631.1 358.7 %all-reduce.15.cloned.1.call-start = ((), (), s32[]{:S(2)}) async-start(), calls=%async_computation.4 | async-start | bytes 524288 | tf_op jit(solution)/shard_map/psum | solution.py:41
  841.5 394.8 %all-reduce.17.cloned.1.call-start = ((), (), s32[]{:S(2)}) async-start(), calls=%async_computation.5 | async-start | bytes 1835008 | tf_op jit(solution)/shard_map/psum | solution.py:47
  1236.2 18.9 %copy-start.2 = (f32[1792,128]{0,1:T(8,128)S(1)}, f32[1792,128]{0,1:T(8,128)}, u32[]{:S(2)}) copy-start(f32[1792,128]{0,1:T(8,128)} %all-reduce.17.cloned.1.call-done) | copy-start | bytes 2752516
Sparse Core Ops, SparseCore 0:
  11.8 153.3 all-reduce.6
  218.8 192.8 all-reduce.8
  429.2 148.1 all-reduce.10
  631.2 192.8 all-reduce.12
  841.6 148.1 all-reduce.14
  1043.6 192.6 all-reduce.16
where the time goes:
time: 1270 us; the launch traced here: 1260 us
  waiting for transfers between devices  1030 us (81%)
  blocking collectives  115 us (9%)
  other arithmetic  76.8 us (6%)
  matrix products  23 us (2%)
  between operations  16.2 us (1%)
    psum x3, waiting for transfers between devices, shards(): right_total = lax.psum(right_partial, ('replica', 'fsdp')) / replicas  578 us
    psum x3, waiting for transfers between devices, shards(): left_total = lax.psum(left_partial, ('replica', 'tensor')) / replicas  451 us
    psum x3, blocking collectives, shards(): lax.psum(gram_of(left_total).astype(jnp.bfloat16), 'fsdp')  74.8 us
    psum x3, blocking collectives, shards(): column_sq = lax.psum(jnp.sum(right_total * right_total, axis=0), 'tensor')  40.2 us
    another operation x9, other arithmetic, orthonormal(): jnp.linalg.cholesky(gram_total + ridge * jnp.eye(rank, dtype=jnp.float32))  37.2 us
    another operation x6, other arithmetic, orthonormal(): lax.linalg.triangular_solve(lower_factor, rows, left_side=False, lower=Tr...  31.4 us
  transfers between devices with their start and end apart: 6, of which 6 were waited for; matrix products, arithmetic and copies ran while one was open for 0% of the time, Pallas kernels for 0%

commit v1 on v0

v1 whole, which is shorter than its diff:
```python
import functools
import math

import jax
import jax.numpy as jnp
from jax import lax
from jax.experimental import pallas as pl
from jax.experimental.pallas import tpu as pltpu
from jax.sharding import PartitionSpec as P

D = 4096
FF = 14336
R = 128
ITERS = 3
NY, NZ, NX = 8, 8, 4
ROWS = 512
COLS = 1792
LY = ROWS // NY
RC = COLS // 2
RZ = RC // NZ

ridge_scale = 1e-06
norm_eps = 1e-06
momentum_decay = 0.95

MESH = pl.DeviceIdType.MESH
f32, bf16 = jnp.float32, jnp.bfloat16
HIGHEST = lax.Precision.HIGHEST


def split3(w):
    high = w.astype(bf16).astype(f32)
    rest = w - high
    mid = rest.astype(bf16).astype(f32)
    return high, mid, rest - mid


def factor_inverse(work):
    size = 16
    sub = lax.broadcasted_iota(jnp.int32, (size, R), 0)
    lane = lax.broadcasted_iota(jnp.int32, (size, R), 1)
    for first in range(0, R, size):
        left, right = work[first : first + size, 0:R], work[first : first + size, R : 2 * R]
        cols = [
            jnp.broadcast_to(left[:, first + k : first + k + 1], (size, R)) for k in range(size)
        ]
        scale = jnp.zeros((size, R), f32)
        for j in range(size):
            pivot = jnp.broadcast_to(cols[j][j : j + 1, :], (size, R))
            scale = jnp.where(sub == j, lax.rsqrt(pivot), scale)
            if j < size - 1:
                ratio = jnp.where(sub > j, cols[j], 0.0) * (1.0 / pivot)
                for k in range(j + 1, size):
                    cols[k] = cols[k] - ratio * cols[k][j : j + 1, :]
                left = left - ratio * left[j : j + 1, :]
                right = right - ratio * right[j : j + 1, :]
        left = jnp.where(lane >= first, left * scale, 0.0)
        right = right * scale
        work[first : first + size, 0:R] = left
        work[first : first + size, R : 2 * R] = right
        below = first + size
        if below < R:
            ph, pm, pw = split3(jnp.concatenate([left, right], 1))
            wh, wm, ww = split3(jnp.where(lane >= below, left, 0.0))
            a = jnp.concatenate([wh, wh, wm, wm, wh, ww], 0).astype(bf16)
            b = jnp.concatenate([ph, pm, ph, pm, pw, ph], 0).astype(bf16)
            update = lax.dot_general(a, b, (((0,), (0,)), ((), ())), preferred_element_type=f32)
            work[below:R, :] = work[below:R, :] - update[below:R, :]


def iterate_kernel(
    m_hbm, q_ref, lr_ref, rr_ref, d_ref,
    m, f, ls, ly, lz, la, gc, gx, gs, work, rcs, rc, rzs, rz, rx, ra, cs, scale,
    m_sem, ly_s, ly_r, lz_s, lz_r, la_s, la_r, gc_s, gc_r, gx_s, gx_r,
    rc_s, rc_r, rz_s, rz_r, rx_s, rx_r, ra_s, ra_r, rm_s, rm_r, cs_s, cs_r,
):
    z, fs, y = lax.axis_index("replica"), lax.axis_index("fsdp"), lax.axis_index("tensor")
    x, c = fs // 2, lax.rem(fs, 2)
    mate = {"fsdp": x * 2 + 1 - c}

    def at_y(k):
        return {"tensor": lax.rem(y + k, NY)}

    def at_z(k):
        return {"replica": lax.rem(z + k, NZ)}

    def at_x(k):
        return {"fsdp": lax.rem(x + k, NX) * 2 + c}

    def copy(src, dst, send, recv, to):
        return pltpu.make_async_remote_copy(
            src_ref=src, dst_ref=dst, send_sem=send, recv_sem=recv, device_id=to, device_id_type=MESH
        )

    load = pltpu.make_async_copy(m_hbm, m, m_sem)
    load.start()
    barrier = pltpu.get_barrier_semaphore()
    for k in range(1, NY):
        pl.semaphore_signal(barrier, inc=1, device_id=at_y(k), device_id_type=MESH)
    for k in range(1, NZ):
        pl.semaphore_signal(barrier, inc=1, device_id=at_z(k), device_id_type=MESH)
    for k in range(1, NX):
        pl.semaphore_signal(barrier, inc=1, device_id=at_x(k), device_id_type=MESH)
    pl.semaphore_signal(barrier, inc=1, device_id=mate, device_id_type=MESH)
    f[...] = q_ref[...]
    scale[...] = jnp.full((8, R), 1.0 / NZ, f32)
    load.wait()
    pl.semaphore_wait(barrier, NY + NZ + NX - 2)

    def column_scale(it):
        for k in range(1, NY):
            s = lax.rem(y + k, NY)
            copy(cs.at[it, s], cs.at[it, s], cs_s.at[k], cs_r.at[it, s], at_y(k)).wait_recv()
        total = cs[it, 0]
        for s in range(1, NY):
            total = total + cs[it, s]
        scale[...] = math.sqrt(FF) / jnp.sqrt(total + norm_eps)

    def iteration(it, carry):
        ls[...] = jnp.dot(m[...], f[...], preferred_element_type=f32).astype(bf16)
        sends = []

        def start(cp):
            cp.start()
            sends.append(cp)

        for k in range(1, NY):
            t = lax.rem(y + k, NY)
            start(copy(ls.at[pl.ds(t * LY, LY)], ly.at[it, y], ly_s.at[k], ly_r.at[it, y], at_y(k)))
        total = ls[pl.ds(y * LY, LY), :].astype(f32)
        for k in range(1, NY):
            s = lax.rem(y + k, NY)
            copy(ly.at[it, s], ly.at[it, s], ly_s.at[k], ly_r.at[it, s], at_y(k)).wait_recv()
            total = total + ly[it, s].astype(f32)
        lz[it, z] = total.astype(bf16)
        for k in range(1, NZ):
            start(copy(lz.at[it, z], lz.at[it, z], lz_s.at[k], lz_r.at[it, z], at_z(k)))

        @pl.when(it > 0)
        def _():
            column_scale(it - 1)
            scale[...] = scale[...] * (1.0 / NZ)

        for k in range(1, NZ):
            s = lax.rem(z + k, NZ)
            copy(lz.at[it, s], lz.at[it, s], lz_s.at[k], lz_r.at[it, s], at_z(k)).wait_recv()
        total = lz[it, 0].astype(f32)
        for s in range(1, NZ):
            total = total + lz[it, s].astype(f32)
        la[it, pl.ds(y * LY, LY), :] = (total * scale[0:1, :]).astype(bf16)
        mine = la.at[it, pl.ds(y * LY, LY)]
        for k in range(1, NY):
            start(copy(mine, mine, la_s.at[k], la_r.at[it, y], at_y(k)))
        for k in range(1, NY):
            s = lax.rem(y + k, NY)
            theirs = la.at[it, pl.ds(s * LY, LY)]
            copy(theirs, theirs, la_s.at[k], la_r.at[it, s], at_y(k)).wait_recv()
        left = la[it]

        def product(half):
            columns = pl.ds(pl.multiple_of(half * RC, 128), RC)
            return lax.dot_general(
                m[:, columns], left, (((0,), (0,)), ((), ())), preferred_element_type=f32
            )

        gs[...] = lax.dot_general(left, left, (((0,), (0,)), ((), ())), preferred_element_type=f32)
        to_gram = copy(gs, gc.at[it], gc_s, gc_r.at[it], mate)
        start(to_gram)
        rcs[...] = product(1 - c)
        to_mate = copy(rcs, rc.at[it], rc_s, rc_r.at[it], mate)
        start(to_mate)
        own = product(c)
        to_gram.wait_recv()
        gx[it, x] = gs[...] + gc[it]
        for k in range(1, NX):
            start(copy(gx.at[it, x], gx.at[it, x], gx_s.at[k], gx_r.at[it, x], at_x(k)))
        to_mate.wait_recv()
        rzs[...] = (own + rc[it]).astype(bf16)
        for k in range(1, NZ):
            t = lax.rem(z + k, NZ)
            start(copy(rzs.at[pl.ds(t * RZ, RZ)], rz.at[it, z], rz_s.at[k], rz_r.at[it, z], at_z(k)))

        for k in range(1, NX):
            s = lax.rem(x + k, NX)
            copy(gx.at[it, s], gx.at[it, s], gx_s.at[k], gx_r.at[it, s], at_x(k)).wait_recv()
        gram = (gx[it, 0] + gx[it, 1]) + (gx[it, 2] + gx[it, 3])
        eye = lax.broadcasted_iota(jnp.int32, (R, R), 0) == lax.broadcasted_iota(
            jnp.int32, (R, R), 1
        )
        ridge = (ridge_scale / R) * jnp.sum(jnp.where(eye, gram, 0.0), keepdims=True)
        work[:, 0:R] = jnp.where(eye, gram + ridge, gram)
        work[:, R : 2 * R] = jnp.where(eye, 1.0, 0.0)
        factor_inverse(work)

        total = rzs[pl.ds(z * RZ, RZ), :].astype(f32)
        for k in range(1, NZ):
            s = lax.rem(z + k, NZ)
            copy(rz.at[it, s], rz.at[it, s], rz_s.at[k], rz_r.at[it, s], at_z(k)).wait_recv()
            total = total + rz[it, s].astype(f32)
        rx[it, x] = total.astype(bf16)
        for k in range(1, NX):
            start(copy(rx.at[it, x], rx.at[it, x], rx_s.at[k], rx_r.at[it, x], at_x(k)))
        for k in range(1, NX):
            s = lax.rem(x + k, NX)
            copy(rx.at[it, s], rx.at[it, s], rx_s.at[k], rx_r.at[it, s], at_x(k)).wait_recv()
        total = (rx[it, 0].astype(f32) + rx[it, 1].astype(f32)) + (
            rx[it, 2].astype(f32) + rx[it, 3].astype(f32)
        )
        right = lax.dot_general(
            total, work[:, R : 2 * R], (((1,), (1,)), ((), ())),
            preferred_element_type=f32, precision=HIGHEST,
        )
        here = c * RC + z * RZ
        ra[it, pl.ds(here, RZ), :] = (right * (1.0 / NZ)).astype(bf16)
        mine = ra.at[it, pl.ds(here, RZ)]
        for k in range(1, NZ):
            start(copy(mine, mine, ra_s.at[k], ra_r.at[it, z], at_z(k)))
        start(copy(mine, mine, rm_s.at[0], rm_r.at[it, z], mate))
        for k in range(1, NZ):
            s = lax.rem(z + k, NZ)
            theirs = ra.at[it, pl.ds(c * RC + s * RZ, RZ)]
            copy(theirs, theirs, ra_s.at[k], ra_r.at[it, s], at_z(k)).wait_recv()
            start(copy(theirs, theirs, rm_s.at[k], rm_r.at[it, s], mate))
        for k in range(NZ):
            s = lax.rem(z + k, NZ)
            theirs = ra.at[it, pl.ds((1 - c) * RC + s * RZ, RZ)]
            copy(theirs, theirs, rm_s.at[k], rm_r.at[it, s], mate).wait_recv()
        factor = ra[it]
        f[...] = factor
        wide = factor.astype(f32)
        cs[it, y] = jnp.broadcast_to(jnp.sum(wide * wide, axis=0, keepdims=True), (8, R))
        for k in range(1, NY):
            start(copy(cs.at[it, y], cs.at[it, y], cs_s.at[k], cs_r.at[it, y], at_y(k)))
        for cp in sends:
            cp.wait_send()
        return carry

    lax.fori_loop(0, ITERS, iteration, 0)
    last = ITERS - 1
    lr_ref[...] = lax.dot_general(
        la[last].astype(f32), work[:, R : 2 * R], (((1,), (1,)), ((), ())),
        preferred_element_type=f32, precision=HIGHEST,
    ).astype(bf16)
    rr_ref[...] = f[...]
    column_scale(last)
    d_ref[...] = scale[...]


def iterate(block, q):
    vmem = pl.BlockSpec(memory_space=pltpu.VMEM)
    dma = pltpu.SemaphoreType.DMA
    n = ITERS
    return pl.pallas_call(
        iterate_kernel,
        out_shape=[
            jax.ShapeDtypeStruct((ROWS, R), bf16),
            jax.ShapeDtypeStruct((COLS, R), bf16),
            jax.ShapeDtypeStruct((8, R), f32),
        ],
        in_specs=[pl.BlockSpec(memory_space=pl.ANY), vmem],
        out_specs=[vmem] * 3,
        scratch_shapes=[
            pltpu.VMEM((ROWS, COLS), bf16),
            pltpu.VMEM((COLS, R), bf16),
            pltpu.VMEM((ROWS, R), bf16),
            pltpu.VMEM((n, NY, LY, R), bf16),
            pltpu.VMEM((n, NZ, LY, R), bf16),
            pltpu.VMEM((n, ROWS, R), bf16),
            pltpu.VMEM((n, R, R), f32),
            pltpu.VMEM((n, NX, R, R), f32),
            pltpu.VMEM((R, R), f32),
            pltpu.VMEM((R, 2 * R), f32),
            pltpu.VMEM((RC, R), f32),
            pltpu.VMEM((n, RC, R), f32),
            pltpu.VMEM((RC, R), bf16),
            pltpu.VMEM((n, NZ, RZ, R), bf16),
            pltpu.VMEM((n, NX, RZ, R), bf16),
            pltpu.VMEM((n, COLS, R), bf16),
            pltpu.VMEM((n, NY, 8, R), f32),
            pltpu.VMEM((8, R), f32),
            dma(()),
            dma((NY,)), dma((n, NY)),
            dma((NZ,)), dma((n, NZ)),
            dma((NY,)), dma((n, NY)),
            dma(()), dma((n,)),
            dma((NX,)), dma((n, NX)),
            dma(()), dma((n,)),
            dma((NZ,)), dma((n, NZ)),
            dma((NX,)), dma((n, NX)),
            dma((NZ,)), dma((n, NZ)),
            dma((NZ,)), dma((n, NZ)),
            dma((NY,)), dma((n, NY)),
        ],
        compiler_params=pltpu.CompilerParams(
            collective_id=0, has_side_effects=True, vmem_limit_bytes=40 << 20
        ),
        cost_estimate=pl.CostEstimate(
            flops=12 * ROWS * COLS * R, bytes_accessed=2 * ROWS * COLS, transcendentals=0
        ),
    )(block, q)


def finish_kernel(m, left, right, scale, m_out, u_out, q_out):
    correction = lax.dot_general(
        left[...], right[...], (((1,), (1,)), ((), ())), preferred_element_type=f32
    )
    m_out[...] = (m[...].astype(f32) - (1.0 - momentum_decay) * correction).astype(bf16)
    u_out[...] = math.sqrt(D) * left[...].astype(f32)

    @pl.when(pl.program_id(0) == 0)
    def _():
        q_out[...] = (right[...].astype(f32) * scale[0:1, :]).astype(bf16)


def finish(block, left, right, scale):
    steps = 4
    rows = ROWS // steps
    return pl.pallas_call(
        finish_kernel,
        grid=(steps,),
        out_shape=[
            jax.ShapeDtypeStruct((ROWS, COLS), bf16),
            jax.ShapeDtypeStruct((ROWS, R), f32),
            jax.ShapeDtypeStruct((COLS, R), bf16),
        ],
        in_specs=[
            pl.BlockSpec((rows, COLS), lambda i: (i, 0)),
            pl.BlockSpec((rows, R), lambda i: (i, 0)),
            pl.BlockSpec((COLS, R), lambda i: (0, 0)),
            pl.BlockSpec((8, R), lambda i: (0, 0)),
        ],
        out_specs=[
            pl.BlockSpec((rows, COLS), lambda i: (i, 0)),
            pl.BlockSpec((rows, R), lambda i: (i, 0)),
            pl.BlockSpec((COLS, R), lambda i: (0, 0)),
        ],
        compiler_params=pltpu.CompilerParams(vmem_limit_bytes=40 << 20),
        cost_estimate=pl.CostEstimate(
            flops=2 * ROWS * COLS * R, bytes_accessed=4 * ROWS * COLS, transcendentals=0
        ),
    )(block, left, right, scale)


def shards(momentum, q_prev):
    block = momentum[0]
    left, right, scale = iterate(block, q_prev)
    momentum_next, update_left, q_next = finish(block, left, right, scale)
    return momentum_next[None], update_left, q_next


def solution(mesh):
    in_specs = (P("replica", "fsdp", "tensor"), P("tensor", None))
    out_specs = (P("replica", "fsdp", "tensor"), P("fsdp", None), P("tensor", None))
    return jax.shard_map(shards, mesh=mesh, in_specs=in_specs, out_specs=out_specs, check_vma=False)
```

time: 1270 us -> 162 us (0.13)
  waiting for transfers between devices: 1030 us -> 0 us
  Pallas kernels: 0 us -> 158 us
  blocking collectives: 115 us -> 0 us
  other arithmetic: 76.8 us -> 0 us
  matrix products: 23 us -> 0 us
  between operations: 16.2 us -> 0.65 us
    psum x6 -> x0, waiting for transfers between devices: 1030 us -> none  [the longest x3 578 us: shards(): right_total = lax.psum(right_partial, ('replica', 'fsdp')) / replicas]
    pallas_call x0 -> x2, Pallas kernels: none -> 158 us  [the longest x1 155 us: iterate(): pl.pallas_call(iterate_kernel, out_shape=[jax.ShapeDtypeStruct((ROWS, R),...]
    psum x6 -> x0, blocking collectives: 115 us -> none  [the longest x3 74.8 us: shards(): lax.psum(gram_of(left_total).astype(jnp.bfloat16), 'fsdp')]
    another operation x15 -> x0, other arithmetic: 68.6 us -> none  [the longest x9 37.2 us: orthonormal(): jnp.linalg.cholesky(gram_total + ridge * jnp.eye(rank, dtype=jnp.float32))]
    dot_general x10 -> x0, matrix products: 18.9 us -> none  [the longest x3 8.04 us: shards(): jnp.dot(local_block, factor_round, preferred_element_type=jnp.float32)]
  transfers between devices with their start and end apart: 6 -> 0, of which waited for: 6 -> 0; matrix products, arithmetic and copies ran while one was open for 0% -> 0% of each run, Pallas kernels for 0% -> 0%
where the time goes in v1:
time: 162 us; the launch traced here: 161 us
  Pallas kernels  158 us (98%)
  local copies, waits for them, and re-layouts  2.51 us (2%)
    pallas_call x1, Pallas kernels, iterate(): pl.pallas_call(iterate_kernel, out_shape=[jax.ShapeDtypeStruct((ROWS, R),...  155 us

profile of v1, /device:TPU:1, one launch (start us, length us, event | category | flops | bytes accessed | tf_op | source)
XLA Modules:
  0.0 161.3 jit_solution(8650730732313841619)
XLA Ops:
  0.6 0.0 copy-start
  0.6 1.5 copy-done
  2.1 0.0 copy-start.1
  2.1 1.0 copy-done.1
  3.1 155.4 %shard_map.49 = (bf16[512,128]{1,0:T(8,128)(2,1)S(1)}, bf16[1792,128]{1,0:T(8,128)(2,1)S(1)}, f32[8,128]{1,0:T(8,128)S(1)}) custom-call(bf16[512,1792]{1,0:T(8,128)(2,1)S(1)} %bitcast.2, bf16[1792,128]{1,0:T(8,128)(2,1)S(1)} %copy-done.1), custom_call_target="tpu_custom_call" | custom-call | flops 1409286144 | bytes 1835008 | tf_op jit(solution)/shard_map/pallas_call | solution.py:253
  158.6 2.7 %shard_map.50 = (bf16[512,1792]{1,0:T(8,128)(2,1)}, f32[512,128]{1,0:T(8,128)}, bf16[1792,128]{1,0:T(8,128)(2,1)}) custom-call(bf16[512,1792]{1,0:T(8,128)(2,1)S(1)} %bitcast.3, bf16[512,128]{1,0:T(8,128)(2,1)S(1)} %get-tuple-element.9.left, bf16[1792,128]{1,0:T(8,128)(2,1)S(1)} %get-tuple-element.10.right, f32[8,128]{1,0:T(8,128)S(1)} %get-tuple-element.11.scale), custom_call_target="tpu_custom_call" | custom-call | flops 234881024 | bytes 3670016 | tf_op jit(solution)/shard_map/pallas_call | solution.py:318
Async XLA Ops:
  0.6 1.5 copy-start
  2.1 1.0 copy-start.1

commit v2 on v1

--- a/solution.py
+++ b/solution.py
@@ -16,6 +16,8 @@
 ROWS = 512
 COLS = 1792
 LY = ROWS // NY
+LZ = ROWS // NZ
+HZ = LZ // 2
 RC = COLS // 2
 RZ = RC // NZ
 
@@ -69,10 +71,10 @@
 
 
 def iterate_kernel(
-    m_hbm, q_ref, lr_ref, rr_ref, d_ref,
-    m, f, ls, ly, lz, la, gc, gx, gs, work, rcs, rc, rzs, rz, rx, ra, cs, scale,
-    m_sem, ly_s, ly_r, lz_s, lz_r, la_s, la_r, gc_s, gc_r, gx_s, gx_r,
-    rc_s, rc_r, rz_s, rz_r, rx_s, rx_r, ra_s, ra_r, rm_s, rm_r, cs_s, cs_r,
+    m_hbm, q_hbm, lr_ref, rr_ref, d_ref,
+    m, f, ms, ring, ls, ly, lz, la, gc, gx, gs, work, rcs, rc, rzs, rz, rx, ra, cy, cz, cc, scale,
+    m_sem, q_sem, ring_s, ring_r, ly_s, ly_r, lz_s, lz_r, la_s, la_r, gc_s, gc_r, gx_s, gx_r,
+    rc_s, rc_r, rz_s, rz_r, rx_s, rx_r, ra_s, ra_r, rm_s, rm_r, cy_s, cy_r, cz_s, cz_r, cc_s, cc_r,
 ):
     z, fs, y = lax.axis_index("replica"), lax.axis_index("fsdp"), lax.axis_index("tensor")
     x, c = fs // 2, lax.rem(fs, 2)
@@ -92,8 +94,10 @@
             src_ref=src, dst_ref=dst, send_sem=send, recv_sem=recv, device_id=to, device_id_type=MESH
         )
 
-    load = pltpu.make_async_copy(m_hbm, m, m_sem)
-    load.start()
+    load_m = pltpu.make_async_copy(m_hbm, m, m_sem)
+    load_m.start()
+    load_q = pltpu.make_async_copy(q_hbm, f, q_sem)
+    load_q.start()
     barrier = pltpu.get_barrier_semaphore()
     for k in range(1, NY):
         pl.semaphore_signal(barrier, inc=1, device_id=at_y(k), device_id_type=MESH)
@@ -102,87 +106,165 @@
     for k in range(1, NX):
         pl.semaphore_signal(barrier, inc=1, device_id=at_x(k), device_id_type=MESH)
     pl.semaphore_signal(barrier, inc=1, device_id=mate, device_id_type=MESH)
-    f[...] = q_ref[...]
     scale[...] = jnp.full((8, R), 1.0 / NZ, f32)
-    load.wait()
+    load_q.wait()
+    load_m.wait()
     pl.semaphore_wait(barrier, NY + NZ + NX - 2)
 
+    def chunk(way, j):
+        return pl.ds(pl.multiple_of(lax.rem(j + 2 * NZ, NZ) * LZ + way * HZ, HZ), HZ)
+
+    def ring_copy(way, step):
+        step_to = 1 if way == 0 else NZ - 1
+        if step == 1:
+            src = m.at[chunk(way, z - 1 if way == 0 else z + 1)]
+        else:
+            src = ring.at[way, step - 2]
+        return copy(src, ring.at[way, step - 1], ring_s.at[way, step - 1],
+                    ring_r.at[way, step - 1], at_z(step_to))
+
+    def ring_step(step):
+        for way in range(2):
+            if step > 1:
+                ring_copy(way, step - 1).wait_recv()
+                own = m[chunk(way, z - step if way == 0 else z + step), :].astype(f32)
+                ring[way, step - 2] = (ring[way, step - 2].astype(f32) + own).astype(bf16)
+            ring_copy(way, step).start()
+
+    def ring_end():
+        for way in range(2):
+            ring_copy(way, NZ - 1).wait_recv()
+            total = ring[way, NZ - 2].astype(f32) + m[chunk(way, z), :].astype(f32)
+            high = total.astype(bf16)
+            ms[way * HZ : (way + 1) * HZ, :] = high
+            ms[LZ + way * HZ : LZ + (way + 1) * HZ, :] = (total - high.astype(f32)).astype(bf16)
+
+    def sums_over_z(it):
+        for k in range(1, NZ):
+            s = lax.rem(z + k, NZ)
+            copy(cz.at[it, s], cz.at[it, s], cz_s.at[k], cz_r.at[it, s], at_z(k)).wait_recv()
+        total = cz[it, 0]
+        for s in range(1, NZ):
+            total = total + cz[it, s]
+        cc[it, 0] = total
+        copy(cc.at[it, 0], cc.at[it, 1], cc_s, cc_r.at[it], mate).start()
+
     def column_scale(it):
+        copy(cc.at[it, 0], cc.at[it, 1], cc_s, cc_r.at[it], mate).wait()
+        scale[...] = math.sqrt(FF) / jnp.sqrt(cc[it, 0] + cc[it, 1] + norm_eps)
+
+    def left_first(it, start):
+        ls[...] = jnp.dot(m[...], f[...], preferred_element_type=f32).astype(bf16)
+        for k in range(1, NY):
+            t = lax.rem(y + k, NY)
+            start(copy(ls.at[pl.ds(t * LY, LY)], ly.at[it, y], ly_s.at[k], ly_r.at[it, y], at_y(k)))
+        ring_step(1)
+        total = ls[pl.ds(y * LY, LY), :].astype(f32)
         for k in range(1, NY):
             s = lax.rem(y + k, NY)
-            copy(cs.at[it, s], cs.at[it, s], cs_s.at[k], cs_r.at[it, s], at_y(k)).wait_recv()
-        total = cs[it, 0]
+            copy(ly.at[it, s], ly.at[it, s], ly_s.at[k], ly_r.at[it, s], at_y(k)).wait_recv()
+            total = total + ly[it, s].astype(f32)
+        lz[z] = total.astype(bf16)
+        for k in range(1, NZ):
+            start(copy(lz.at[z], lz.at[z], lz_s.at[k], lz_r.at[z], at_z(k)))
+        ring_step(2)
+        for k in range(1, NZ):
+            s = lax.rem(z + k, NZ)
+            copy(lz.at[s], lz.at[s], lz_s.at[k], lz_r.at[s], at_z(k)).wait_recv()
+        total = lz[0].astype(f32)
+        for s in range(1, NZ):
+            total = total + lz[s].astype(f32)
+        la[it, pl.ds(y * LY, LY), :] = (total * scale[0:1, :]).astype(bf16)
+        mine = la.at[it, pl.ds(y * LY, LY)]
+        for k in range(1, NY):
+            start(copy(mine, mine, la_s.at[k], la_r.at[it, y], at_y(k)))
+        ring_step(3)
+        for k in range(1, NY):
+            s = lax.rem(y + k, NY)
+            theirs = la.at[it, pl.ds(s * LY, LY)]
+            copy(theirs, theirs, la_s.at[k], la_r.at[it, s], at_y(k)).wait_recv()
+
+    def left_later(it, start):
+        both = jnp.dot(ms[...], f[...], preferred_element_type=f32)
+        ly[it, y] = (both[0:LZ, :] + both[LZ : 2 * LZ, :]).astype(bf16)
+        for k in range(1, NY):
+            start(copy(ly.at[it, y], ly.at[it, y], ly_s.at[k], ly_r.at[it, y], at_y(k)))
+        sums_over_z(it - 1)
+        for k in range(1, NY):
+            s = lax.rem(y + k, NY)
+            copy(ly.at[it, s], ly.at[it, s], ly_s.at[k], ly_r.at[it, s], at_y(k)).wait_recv()
+        column_scale(it - 1)
+        total = ly[it, 0].astype(f32)
         for s in range(1, NY):
-            total = total + cs[it, s]
-        scale[...] = math.sqrt(FF) / jnp.sqrt(total + norm_eps)
-
-    def iteration(it, carry):
-        ls[...] = jnp.dot(m[...], f[...], preferred_element_type=f32).astype(bf16)
+            total = total + ly[it, s].astype(f32)
+        rows = (total * (scale[0:1, :] * (1.0 / NZ))).astype(bf16)
+        la[it, pl.ds(z * LZ, LZ), :] = rows
+        mine = la.at[it, pl.ds(z * LZ, LZ)]
+        for k in range(1, NZ):
+            start(copy(mine, mine, la_s.at[k], la_r.at[it, z], at_z(k)))
+        return rows
+
+    def wait_left_later(it):
+        for k in range(1, NZ):
+            s = lax.rem(z + k, NZ)
+            theirs = la.at[it, pl.ds(s * LZ, LZ)]
+            copy(theirs, theirs, la_s.at[k], la_r.at[it, s], at_z(k)).wait_recv()
+
+    def product(block, left, half):
+        columns = pl.ds(pl.multiple_of(half * RC, 128), RC)
+        return lax.dot_general(
+            block[:, columns], left, (((0,), (0,)), ((), ())), preferred_element_type=f32
+        )
+
+    def iteration(it, first):
         sends = []
 
         def start(cp):
             cp.start()
             sends.append(cp)
 
-        for k in range(1, NY):
-            t = lax.rem(y + k, NY)
-            start(copy(ls.at[pl.ds(t * LY, LY)], ly.at[it, y], ly_s.at[k], ly_r.at[it, y], at_y(k)))
-        total = ls[pl.ds(y * LY, LY), :].astype(f32)
-        for k in range(1, NY):
-            s = lax.rem(y + k, NY)
-            copy(ly.at[it, s], ly.at[it, s], ly_s.at[k], ly_r.at[it, s], at_y(k)).wait_recv()
-            total = total + ly[it, s].astype(f32)
-        lz[it, z] = total.astype(bf16)
-        for k in range(1, NZ):
-            start(copy(lz.at[it, z], lz.at[it, z], lz_s.at[k], lz_r.at[it, z], at_z(k)))
-
-        @pl.when(it > 0)
-        def _():
-            column_scale(it - 1)
-            scale[...] = scale[...] * (1.0 / NZ)
-
-        for k in range(1, NZ):
-            s = lax.rem(z + k, NZ)
-            copy(lz.at[it, s], lz.at[it, s], lz_s.at[k], lz_r.at[it, s], at_z(k)).wait_recv()
-        total = lz[it, 0].astype(f32)
-        for s in range(1, NZ):
-            total = total + lz[it, s].astype(f32)
-        la[it, pl.ds(y * LY, LY), :] = (total * scale[0:1, :]).astype(bf16)
-        mine = la.at[it, pl.ds(y * LY, LY)]
-        for k in range(1, NY):
-            start(copy(mine, mine, la_s.at[k], la_r.at[it, y], at_y(k)))
-        for k in range(1, NY):
-            s = lax.rem(y + k, NY)
-            theirs = la.at[it, pl.ds(s * LY, LY)]
-            copy(theirs, theirs, la_s.at[k], la_r.at[it, s], at_y(k)).wait_recv()
-        left = la[it]
-
-        def product(half):
-            columns = pl.ds(pl.multiple_of(half * RC, 128), RC)
-            return lax.dot_general(
-                m[:, columns], left, (((0,), (0,)), ((), ())), preferred_element_type=f32
+        def gram_to_mate():
+            left = la[it]
+            gs[...] = lax.dot_general(
+                left, left, (((0,), (0,)), ((), ())), preferred_element_type=f32
             )
-
-        gs[...] = lax.dot_general(left, left, (((0,), (0,)), ((), ())), preferred_element_type=f32)
-        to_gram = copy(gs, gc.at[it], gc_s, gc_r.at[it], mate)
-        start(to_gram)
-        rcs[...] = product(1 - c)
+            start(copy(gs, gc.at[it], gc_s, gc_r.at[it], mate))
+
+        def gram_over_x():
+            copy(gs, gc.at[it], gc_s, gc_r.at[it], mate).wait_recv()
+            gx[it, x] = gs[...] + gc[it]
+            for k in range(1, NX):
+                start(copy(gx.at[it, x], gx.at[it, x], gx_s.at[k], gx_r.at[it, x], at_x(k)))
+
+        if first:
+            left_first(it, start)
+            ring_step(4)
+            gram_to_mate()
+            block, rows = m, la[it]
+        else:
+            rows = left_later(it, start)
+            block, rows = ms, jnp.concatenate([rows, rows], 0)
+        rcs[...] = product(block, rows, 1 - c)
         to_mate = copy(rcs, rc.at[it], rc_s, rc_r.at[it], mate)
         start(to_mate)
-        own = product(c)
-        to_gram.wait_recv()
-        gx[it, x] = gs[...] + gc[it]
-        for k in range(1, NX):
-            start(copy(gx.at[it, x], gx.at[it, x], gx_s.at[k], gx_r.at[it, x], at_x(k)))
+        own = product(block, rows, c)
+        if first:
+            gram_over_x()
         to_mate.wait_recv()
         rzs[...] = (own + rc[it]).astype(bf16)
         for k in range(1, NZ):
             t = lax.rem(z + k, NZ)
             start(copy(rzs.at[pl.ds(t * RZ, RZ)], rz.at[it, z], rz_s.at[k], rz_r.at[it, z], at_z(k)))
+        if not first:
+            wait_left_later(it)
+            gram_to_mate()
+            gram_over_x()
 
         for k in range(1, NX):
             s = lax.rem(x + k, NX)
             copy(gx.at[it, s], gx.at[it, s], gx_s.at[k], gx_r.at[it, s], at_x(k)).wait_recv()
+        if first:
+            ring_step(5)
         gram = (gx[it, 0] + gx[it, 1]) + (gx[it, 2] + gx[it, 3])
         eye = lax.broadcasted_iota(jnp.int32, (R, R), 0) == lax.broadcasted_iota(
             jnp.int32, (R, R), 1
@@ -200,6 +282,8 @@
         rx[it, x] = total.astype(bf16)
         for k in range(1, NX):
             start(copy(rx.at[it, x], rx.at[it, x], rx_s.at[k], rx_r.at[it, x], at_x(k)))
+        if first:
+            ring_step(6)
         for k in range(1, NX):
             s = lax.rem(x + k, NX)
             copy(rx.at[it, s], rx.at[it, s], rx_s.at[k], rx_r.at[it, s], at_x(k)).wait_recv()
@@ -209,45 +293,67 @@
         right = lax.dot_general(
             total, work[:, R : 2 * R], (((1,), (1,)), ((), ())),
             preferred_element_type=f32, precision=HIGHEST,
-        )
+        ) * (1.0 / NZ)
         here = c * RC + z * RZ
-        ra[it, pl.ds(here, RZ), :] = (right * (1.0 / NZ)).astype(bf16)
+        ra[it, pl.ds(here, RZ), :] = right.astype(bf16)
         mine = ra.at[it, pl.ds(here, RZ)]
         for k in range(1, NZ):
             start(copy(mine, mine, ra_s.at[k], ra_r.at[it, z], at_z(k)))
+        cy[it, y] = jnp.broadcast_to(jnp.sum(right * right, axis=0, keepdims=True), (8, R))
+        for k in range(1, NY):
+            start(copy(cy.at[it, y], cy.at[it, y], cy_s.at[k], cy_r.at[it, y], at_y(k)))
         start(copy(mine, mine, rm_s.at[0], rm_r.at[it, z], mate))
-        for k in range(1, NZ):
+        if first:
+            ring_step(7)
+        for k in range(1, NY):
+            s = lax.rem(y + k, NY)
+            copy(cy.at[it, s], cy.at[it, s], cy_s.at[k], cy_r.at[it, s], at_y(k)).wait_recv()
+        total = cy[it, 0]
+        for s in range(1, NY):
+            total = total + cy[it, s]
+        cz[it, z] = total
+        for k in range(1, NZ):
+            start(copy(cz.at[it, z], cz.at[it, z], cz_s.at[k], cz_r.at[it, z], at_z(k)))
+        for k in (1, 7, 2, 6, 3, 5, 4):
             s = lax.rem(z + k, NZ)
             theirs = ra.at[it, pl.ds(c * RC + s * RZ, RZ)]
             copy(theirs, theirs, ra_s.at[k], ra_r.at[it, s], at_z(k)).wait_recv()
             start(copy(theirs, theirs, rm_s.at[k], rm_r.at[it, s], mate))
+        if first:
+            ring_end()
         for k in range(NZ):
             s = lax.rem(z + k, NZ)
             theirs = ra.at[it, pl.ds((1 - c) * RC + s * RZ, RZ)]
             copy(theirs, theirs, rm_s.at[k], rm_r.at[it, s], mate).wait_recv()
-        factor = ra[it]
-        f[...] = factor
-        wide = factor.astype(f32)
-        cs[it, y] = jnp.broadcast_to(jnp.sum(wide * wide, axis=0, keepdims=True), (8, R))
-        for k in range(1, NY):
-            start(copy(cs.at[it, y], cs.at[it, y], cs_s.at[k], cs_r.at[it, y], at_y(k)))
+        f[...] = ra[it]
         for cp in sends:
             cp.wait_send()
+        if first:
+            for way in range(2):
+                for step in range(1, NZ):
+                    ring_copy(way, step).wait_send()
+
+    iteration(0, True)
+
+    def again(it, carry):
+        iteration(it, False)
         return carry
 
-    lax.fori_loop(0, ITERS, iteration, 0)
+    lax.fori_loop(1, ITERS, again, 0)
     last = ITERS - 1
     lr_ref[...] = lax.dot_general(
         la[last].astype(f32), work[:, R : 2 * R], (((1,), (1,)), ((), ())),
         preferred_element_type=f32, precision=HIGHEST,
     ).astype(bf16)
     rr_ref[...] = f[...]
+    sums_over_z(last)
     column_scale(last)
     d_ref[...] = scale[...]
 
 
 def iterate(block, q):
     vmem = pl.BlockSpec(memory_space=pltpu.VMEM)
+    hbm = pl.BlockSpec(memory_space=pltpu.HBM)
     dma = pltpu.SemaphoreType.DMA
     n = ITERS
     return pl.pallas_call(
@@ -257,14 +363,16 @@
             jax.ShapeDtypeStruct((COLS, R), bf16),
             jax.ShapeDtypeStruct((8, R), f32),
         ],
-        in_specs=[pl.BlockSpec(memory_space=pl.ANY), vmem],
+        in_specs=[hbm, hbm],
         out_specs=[vmem] * 3,
         scratch_shapes=[
             pltpu.VMEM((ROWS, COLS), bf16),
             pltpu.VMEM((COLS, R), bf16),
+            pltpu.VMEM((2 * LZ, COLS), bf16),
+            pltpu.VMEM((2, NZ - 1, HZ, COLS), bf16),
             pltpu.VMEM((ROWS, R), bf16),
             pltpu.VMEM((n, NY, LY, R), bf16),
-            pltpu.VMEM((n, NZ, LY, R), bf16),
+            pltpu.VMEM((NZ, LY, R), bf16),
             pltpu.VMEM((n, ROWS, R), bf16),
             pltpu.VMEM((n, R, R), f32),
             pltpu.VMEM((n, NX, R, R), f32),
@@ -277,10 +385,13 @@
             pltpu.VMEM((n, NX, RZ, R), bf16),
             pltpu.VMEM((n, COLS, R), bf16),
             pltpu.VMEM((n, NY, 8, R), f32),
+            pltpu.VMEM((n, NZ, 8, R), f32),
+            pltpu.VMEM((n, 2, 8, R), f32),
             pltpu.VMEM((8, R), f32),
-            dma(()),
+            dma(()), dma(()),
+            dma((2, NZ - 1)), dma((2, NZ - 1)),
             dma((NY,)), dma((n, NY)),
-            dma((NZ,)), dma((n, NZ)),
+            dma((NZ,)), dma((NZ,)),
             dma((NY,)), dma((n, NY)),
             dma(()), dma((n,)),
             dma((NX,)), dma((n, NX)),
@@ -290,9 +401,11 @@
             dma((NZ,)), dma((n, NZ)),
             dma((NZ,)), dma((n, NZ)),
             dma((NY,)), dma((n, NY)),
+            dma((NZ,)), dma((n, NZ)),
+            dma(()), dma((n,)),
         ],
         compiler_params=pltpu.CompilerParams(
-            collective_id=0, has_side_effects=True, vmem_limit_bytes=40 << 20
+            collective_id=0, has_side_effects=True, vmem_limit_bytes=56 << 20
         ),
         cost_estimate=pl.CostEstimate(
             flops=12 * ROWS * COLS * R, bytes_accessed=2 * ROWS * COLS, transcendentals=0
@@ -334,7 +447,7 @@
             pl.BlockSpec((rows, R), lambda i: (i, 0)),
             pl.BlockSpec((COLS, R), lambda i: (0, 0)),
         ],
-        compiler_params=pltpu.CompilerParams(vmem_limit_bytes=40 << 20),
+        compiler_params=pltpu.CompilerParams(vmem_limit_bytes=56 << 20),
         cost_estimate=pl.CostEstimate(
             flops=2 * ROWS * COLS * R, bytes_accessed=4 * ROWS * COLS, transcendentals=0
         ),

time: 162 us -> 143 us (0.88)
  Pallas kernels: 158 us -> 142 us
  local copies, waits for them, and re-layouts: 2.51 us -> 0 us
    pallas_call x1, Pallas kernels: 155 us -> 137 us  [iterate(): pl.pallas_call(iterate_kernel, out_shape=[jax.ShapeDtypeStruct((ROWS, R),...]
    unnamed x4 -> x0, local copies, waits for them, and re-layouts: 2.51 us -> none
    pallas_call x1, Pallas kernels: 2.72 us -> 4.63 us  [finish(): pl.pallas_call(finish_kernel, grid=(steps,), out_shape=[jax.ShapeDtypeStr...]
where the time goes in v2:
time: 143 us; the launch traced here: 142 us
  Pallas kernels  142 us (99%)
    pallas_call x1, Pallas kernels, iterate(): pl.pallas_call(iterate_kernel, out_shape=[jax.ShapeDtypeStruct((ROWS, R),...  137 us
    pallas_call x1, Pallas kernels, finish(): pl.pallas_call(finish_kernel, grid=(steps,), out_shape=[jax.ShapeDtypeStr...  4.63 us

profile of v2, /device:TPU:1, one launch (start us, length us, event | category | flops | bytes accessed | tf_op | source)
XLA Modules:
  0.0 142.5 jit_solution(15531213466665931518)
XLA Ops:
  0.6 137.2 %shard_map.49 = (bf16[512,128]{1,0:T(8,128)(2,1)}, bf16[1792,128]{1,0:T(8,128)(2,1)}, f32[8,128]{1,0:T(8,128)}) custom-call(bf16[512,1792]{1,0:T(8,128)(2,1)} %bitcast.2, bf16[1792,128]{1,0:T(8,128)(2,1)} %q_hbm.1), custom_call_target="tpu_custom_call" | custom-call | flops 1409286144 | bytes 1835008 | tf_op jit(solution)/shard_map/pallas_call | solution.py:359
  137.8 4.6 %shard_map.50 = (bf16[512,1792]{1,0:T(8,128)(2,1)}, f32[512,128]{1,0:T(8,128)}, bf16[1792,128]{1,0:T(8,128)(2,1)}) custom-call(bf16[512,1792]{1,0:T(8,128)(2,1)} %bitcast.3, bf16[512,128]{1,0:T(8,128)(2,1)} %get-tuple-element.9.left, bf16[1792,128]{1,0:T(8,128)(2,1)} %get-tuple-element.10.right, f32[8,128]{1,0:T(8,128)} %get-tuple-element.11.scale), custom_call_target="tpu_custom_call" | custom-call | flops 234881024 | bytes 3670016 | tf_op jit(solution)/shard_map/pallas_call | solution.py:431

commit v3 on v2

--- a/solution.py
+++ b/solution.py
@@ -20,6 +20,7 @@
 HZ = LZ // 2
 RC = COLS // 2
 RZ = RC // NZ
+PARTS = ((0, 112),)
 
 ridge_scale = 1e-06
 norm_eps = 1e-06
@@ -109,6 +110,7 @@
     scale[...] = jnp.full((8, R), 1.0 / NZ, f32)
     load_q.wait()
     load_m.wait()
+    ls[...] = jnp.dot(m[...], f[...], preferred_element_type=f32).astype(bf16)
     pl.semaphore_wait(barrier, NY + NZ + NX - 2)
 
     def chunk(way, j):
@@ -154,7 +156,6 @@
         scale[...] = math.sqrt(FF) / jnp.sqrt(cc[it, 0] + cc[it, 1] + norm_eps)
 
     def left_first(it, start):
-        ls[...] = jnp.dot(m[...], f[...], preferred_element_type=f32).astype(bf16)
         for k in range(1, NY):
             t = lax.rem(y + k, NY)
             start(copy(ls.at[pl.ds(t * LY, LY)], ly.at[it, y], ly_s.at[k], ly_r.at[it, y], at_y(k)))
@@ -214,7 +215,7 @@
         columns = pl.ds(pl.multiple_of(half * RC, 128), RC)
         return lax.dot_general(
             block[:, columns], left, (((0,), (0,)), ((), ())), preferred_element_type=f32
-        )
+        ).reshape(NZ, RZ, R)
 
     def iteration(it, first):
         sends = []
@@ -232,7 +233,7 @@
 
         def gram_over_x():
             copy(gs, gc.at[it], gc_s, gc_r.at[it], mate).wait_recv()
-            gx[it, x] = gs[...] + gc[it]
+            gx[it, x] = (gs[...] + gc[it]).astype(bf16)
             for k in range(1, NX):
                 start(copy(gx.at[it, x], gx.at[it, x], gx_s.at[k], gx_r.at[it, x], at_x(k)))
 
@@ -244,28 +245,53 @@
         else:
             rows = left_later(it, start)
             block, rows = ms, jnp.concatenate([rows, rows], 0)
+
         rcs[...] = product(block, rows, 1 - c)
-        to_mate = copy(rcs, rc.at[it], rc_s, rc_r.at[it], mate)
-        start(to_mate)
+        to_mate = []
+        for p, (row, size) in enumerate(PARTS):
+            part = pl.ds(row, size)
+            cp = copy(rcs.at[:, part], rc.at[it, :, part], rc_s.at[p], rc_r.at[it, p], mate)
+            start(cp)
+            to_mate.append(cp)
         own = product(block, rows, c)
         if first:
             gram_over_x()
-        to_mate.wait_recv()
-        rzs[...] = (own + rc[it]).astype(bf16)
-        for k in range(1, NZ):
-            t = lax.rem(z + k, NZ)
-            start(copy(rzs.at[pl.ds(t * RZ, RZ)], rz.at[it, z], rz_s.at[k], rz_r.at[it, z], at_z(k)))
-        if not first:
+        for p, (row, size) in enumerate(PARTS):
+            part = pl.ds(row, size)
+            to_mate[p].wait_recv()
+            rzs[:, part] = (own[:, row : row + size] + rc[it, :, part]).astype(bf16)
+            for k in range(1, NZ):
+                t = lax.rem(z + k, NZ)
+                start(copy(rzs.at[t, part], rz.at[it, z, part],
+                           rz_s.at[p, k], rz_r.at[it, p, z], at_z(k)))
+        if first:
+            ring_step(5)
+        else:
             wait_left_later(it)
             gram_to_mate()
             gram_over_x()
 
+        for p, (row, size) in enumerate(PARTS):
+            part = pl.ds(row, size)
+            total = rzs[z, part].astype(f32)
+            for k in range(1, NZ):
+                s = lax.rem(z + k, NZ)
+                there = rz.at[it, s, part]
+                copy(there, there, rz_s.at[p, k], rz_r.at[it, p, s], at_z(k)).wait_recv()
+                total = total + rz[it, s, part].astype(f32)
+            rx[it, x, part] = total.astype(bf16)
+            here = rx.at[it, x, part]
+            for k in range(1, NX):
+                start(copy(here, here, rx_s.at[p, k], rx_r.at[it, p, x], at_x(k)))
+        if first:
+            ring_step(6)
+
         for k in range(1, NX):
             s = lax.rem(x + k, NX)
             copy(gx.at[it, s], gx.at[it, s], gx_s.at[k], gx_r.at[it, s], at_x(k)).wait_recv()
-        if first:
-            ring_step(5)
-        gram = (gx[it, 0] + gx[it, 1]) + (gx[it, 2] + gx[it, 3])
+        gram = (gx[it, 0].astype(f32) + gx[it, 1].astype(f32)) + (
+            gx[it, 2].astype(f32) + gx[it, 3].astype(f32)
+        )
         eye = lax.broadcasted_iota(jnp.int32, (R, R), 0) == lax.broadcasted_iota(
             jnp.int32, (R, R), 1
         )
@@ -274,35 +300,28 @@
         work[:, R : 2 * R] = jnp.where(eye, 1.0, 0.0)
         factor_inverse(work)
 
-        total = rzs[pl.ds(z * RZ, RZ), :].astype(f32)
-        for k in range(1, NZ):
-            s = lax.rem(z + k, NZ)
-            copy(rz.at[it, s], rz.at[it, s], rz_s.at[k], rz_r.at[it, s], at_z(k)).wait_recv()
-            total = total + rz[it, s].astype(f32)
-        rx[it, x] = total.astype(bf16)
-        for k in range(1, NX):
-            start(copy(rx.at[it, x], rx.at[it, x], rx_s.at[k], rx_r.at[it, x], at_x(k)))
-        if first:
-            ring_step(6)
-        for k in range(1, NX):
-            s = lax.rem(x + k, NX)
-            copy(rx.at[it, s], rx.at[it, s], rx_s.at[k], rx_r.at[it, s], at_x(k)).wait_recv()
-        total = (rx[it, 0].astype(f32) + rx[it, 1].astype(f32)) + (
-            rx[it, 2].astype(f32) + rx[it, 3].astype(f32)
-        )
-        right = lax.dot_general(
-            total, work[:, R : 2 * R], (((1,), (1,)), ((), ())),
-            preferred_element_type=f32, precision=HIGHEST,
-        ) * (1.0 / NZ)
-        here = c * RC + z * RZ
-        ra[it, pl.ds(here, RZ), :] = right.astype(bf16)
-        mine = ra.at[it, pl.ds(here, RZ)]
-        for k in range(1, NZ):
-            start(copy(mine, mine, ra_s.at[k], ra_r.at[it, z], at_z(k)))
-        cy[it, y] = jnp.broadcast_to(jnp.sum(right * right, axis=0, keepdims=True), (8, R))
+        squares = jnp.zeros((1, R), f32)
+        for p, (row, size) in enumerate(PARTS):
+            part = pl.ds(row, size)
+            for k in range(1, NX):
+                s = lax.rem(x + k, NX)
+                there = rx.at[it, s, part]
+                copy(there, there, rx_s.at[p, k], rx_r.at[it, p, s], at_x(k)).wait_recv()
+            total = (rx[it, 0, part].astype(f32) + rx[it, 1, part].astype(f32)) + (
+                rx[it, 2, part].astype(f32) + rx[it, 3, part].astype(f32)
+            )
+            right = lax.dot_general(
+                total, work[:, R : 2 * R], (((1,), (1,)), ((), ())),
+                preferred_element_type=f32, precision=HIGHEST,
+            ) * (1.0 / NZ)
+            ra[it, c, z, part] = right.astype(bf16)
+            mine = ra.at[it, c, z, part]
+            for k in range(1, NZ):
+                start(copy(mine, mine, ra_s.at[p, k], ra_r.at[it, p, z], at_z(k)))
+            squares = squares + jnp.sum(right * right, axis=0, keepdims=True)
+        cy[it, y] = jnp.broadcast_to(squares, (8, R))
         for k in range(1, NY):
             start(copy(cy.at[it, y], cy.at[it, y], cy_s.at[k], cy_r.at[it, y], at_y(k)))
-        start(copy(mine, mine, rm_s.at[0], rm_r.at[it, z], mate))
         if first:
             ring_step(7)
         for k in range(1, NY):
@@ -314,18 +333,20 @@
         cz[it, z] = total
         for k in range(1, NZ):
             start(copy(cz.at[it, z], cz.at[it, z], cz_s.at[k], cz_r.at[it, z], at_z(k)))
-        for k in (1, 7, 2, 6, 3, 5, 4):
-            s = lax.rem(z + k, NZ)
-            theirs = ra.at[it, pl.ds(c * RC + s * RZ, RZ)]
-            copy(theirs, theirs, ra_s.at[k], ra_r.at[it, s], at_z(k)).wait_recv()
-            start(copy(theirs, theirs, rm_s.at[k], rm_r.at[it, s], mate))
+        for p, (row, size) in enumerate(PARTS):
+            part = pl.ds(row, size)
+            for k in range(1, NZ):
+                s = lax.rem(z + k, NZ)
+                there = ra.at[it, c, s, part]
+                copy(there, there, ra_s.at[p, k], ra_r.at[it, p, s], at_z(k)).wait_recv()
+            half = ra.at[it, c, :, part]
+            start(copy(half, half, rm_s.at[p], rm_r.at[it, p], mate))
         if first:
             ring_end()
-        for k in range(NZ):
-            s = lax.rem(z + k, NZ)
-            theirs = ra.at[it, pl.ds((1 - c) * RC + s * RZ, RZ)]
-            copy(theirs, theirs, rm_s.at[k], rm_r.at[it, s], mate).wait_recv()
-        f[...] = ra[it]
+        for p, (row, size) in enumerate(PARTS):
+            half = ra.at[it, 1 - c, :, pl.ds(row, size)]
+            copy(half, half, rm_s.at[p], rm_r.at[it, p], mate).wait_recv()
+        f[...] = ra[it].reshape(COLS, R)
         for cp in sends:
             cp.wait_send()
         if first:
@@ -355,7 +376,7 @@
     vmem = pl.BlockSpec(memory_space=pltpu.VMEM)
     hbm = pl.BlockSpec(memory_space=pltpu.HBM)
     dma = pltpu.SemaphoreType.DMA
-    n = ITERS
+    n, parts = ITERS, len(PARTS)
     return pl.pallas_call(
         iterate_kernel,
         out_shape=[
@@ -375,15 +396,15 @@
             pltpu.VMEM((NZ, LY, R), bf16),
             pltpu.VMEM((n, ROWS, R), bf16),
             pltpu.VMEM((n, R, R), f32),
-            pltpu.VMEM((n, NX, R, R), f32),
+            pltpu.VMEM((n, NX, R, R), bf16),
             pltpu.VMEM((R, R), f32),
             pltpu.VMEM((R, 2 * R), f32),
-            pltpu.VMEM((RC, R), f32),
-            pltpu.VMEM((n, RC, R), f32),
-            pltpu.VMEM((RC, R), bf16),
+            pltpu.VMEM((NZ, RZ, R), f32),
+            pltpu.VMEM((n, NZ, RZ, R), f32),
+            pltpu.VMEM((NZ, RZ, R), bf16),
             pltpu.VMEM((n, NZ, RZ, R), bf16),
             pltpu.VMEM((n, NX, RZ, R), bf16),
-            pltpu.VMEM((n, COLS, R), bf16),
+            pltpu.VMEM((n, 2, NZ, RZ, R), bf16),
             pltpu.VMEM((n, NY, 8, R), f32),
             pltpu.VMEM((n, NZ, 8, R), f32),
             pltpu.VMEM((n, 2, 8, R), f32),
@@ -395,11 +416,11 @@
             dma((NY,)), dma((n, NY)),
             dma(()), dma((n,)),
             dma((NX,)), dma((n, NX)),
-            dma(()), dma((n,)),
-            dma((NZ,)), dma((n, NZ)),
-            dma((NX,)), dma((n, NX)),
-            dma((NZ,)), dma((n, NZ)),
-            dma((NZ,)), dma((n, NZ)),
+            dma((parts,)), dma((n, parts)),
+            dma((parts, NZ)), dma((n, parts, NZ)),
+            dma((parts, NX)), dma((n, parts, NX)),
+            dma((parts, NZ)), dma((n, parts, NZ)),
+            dma((parts,)), dma((n, parts)),
             dma((NY,)), dma((n, NY)),
             dma((NZ,)), dma((n, NZ)),
             dma(()), dma((n,)),
@@ -426,7 +447,7 @@
 
 
 def finish(block, left, right, scale):
-    steps = 4
+    steps = 2
     rows = ROWS // steps
     return pl.pallas_call(
         finish_kernel,

time: 143 us -> 132 us (0.923)
  Pallas kernels: 142 us -> 132 us
    pallas_call x1, Pallas kernels: 137 us -> 128 us  [iterate(): pl.pallas_call(iterate_kernel, out_shape=[jax.ShapeDtypeStruct((ROWS, R),...]
where the time goes in v3:
time: 132 us
  Pallas kernels  132 us (100%)
    pallas_call x1, Pallas kernels, iterate(): pl.pallas_call(iterate_kernel, out_shape=[jax.ShapeDtypeStruct((ROWS, R),...  128 us
    pallas_call x1, Pallas kernels, finish(): pl.pallas_call(finish_kernel, grid=(steps,), out_shape=[jax.ShapeDtypeStr...  3.38 us

profile of v3, /device:TPU:1, one launch (start us, length us, event | category | flops | bytes accessed | tf_op | source)
XLA Modules:
  0.0 132.3 jit_solution(15430269775376440340)
XLA Ops:
  0.6 128.3 %shard_map.49 = (bf16[512,128]{1,0:T(8,128)(2,1)}, bf16[1792,128]{1,0:T(8,128)(2,1)}, f32[8,128]{1,0:T(8,128)}) custom-call(bf16[512,1792]{1,0:T(8,128)(2,1)} %bitcast.2, bf16[1792,128]{1,0:T(8,128)(2,1)} %q_hbm.1), custom_call_target="tpu_custom_call" | custom-call | flops 1409286144 | bytes 1835008 | tf_op jit(solution)/shard_map/pallas_call | solution.py:380
  128.9 3.4 %shard_map.50 = (bf16[512,1792]{1,0:T(8,128)(2,1)}, f32[512,128]{1,0:T(8,128)}, bf16[1792,128]{1,0:T(8,128)(2,1)}) custom-call(bf16[512,1792]{1,0:T(8,128)(2,1)} %bitcast.3, bf16[512,128]{1,0:T(8,128)(2,1)} %get-tuple-element.9.left, bf16[1792,128]{1,0:T(8,128)(2,1)} %get-tuple-element.10.right, f32[8,128]{1,0:T(8,128)} %get-tuple-element.11.scale), custom_call_target="tpu_custom_call" | custom-call | flops 234881024 | bytes 3670016 | tf_op jit(solution)/shard_map/pallas_call | solution.py:452

commit v4 on v2

--- a/solution.py
+++ b/solution.py
@@ -20,6 +20,8 @@
 HZ = LZ // 2
 RC = COLS // 2
 RZ = RC // NZ
+RING = (4, 3, 5, 2, 6, 1, 7)
+RING_X = (2, 1, 3)
 
 ridge_scale = 1e-06
 norm_eps = 1e-06
@@ -72,7 +74,7 @@
 
 def iterate_kernel(
     m_hbm, q_hbm, lr_ref, rr_ref, d_ref,
-    m, f, ms, ring, ls, ly, lz, la, gc, gx, gs, work, rcs, rc, rzs, rz, rx, ra, cy, cz, cc, scale,
+    m, ms, ring, ls, ly, lz, la, gc, gx, gs, work, rcs, rc, rzs, rz, rx, ra, cy, cz, cc, scale,
     m_sem, q_sem, ring_s, ring_r, ly_s, ly_r, lz_s, lz_r, la_s, la_r, gc_s, gc_r, gx_s, gx_r,
     rc_s, rc_r, rz_s, rz_r, rx_s, rx_r, ra_s, ra_r, rm_s, rm_r, cy_s, cy_r, cz_s, cz_r, cc_s, cc_r,
 ):
@@ -94,9 +96,12 @@
             src_ref=src, dst_ref=dst, send_sem=send, recv_sem=recv, device_id=to, device_id_type=MESH
         )
 
+    def factor(it):
+        return ra[it].reshape(COLS, R)
+
     load_m = pltpu.make_async_copy(m_hbm, m, m_sem)
     load_m.start()
-    load_q = pltpu.make_async_copy(q_hbm, f, q_sem)
+    load_q = pltpu.make_async_copy(q_hbm, ra.at[0], q_sem)
     load_q.start()
     barrier = pltpu.get_barrier_semaphore()
     for k in range(1, NY):
@@ -109,6 +114,7 @@
     scale[...] = jnp.full((8, R), 1.0 / NZ, f32)
     load_q.wait()
     load_m.wait()
+    ls[...] = jnp.dot(m[...], factor(0), preferred_element_type=f32).astype(bf16)
     pl.semaphore_wait(barrier, NY + NZ + NX - 2)
 
     def chunk(way, j):
@@ -139,8 +145,14 @@
             ms[way * HZ : (way + 1) * HZ, :] = high
             ms[LZ + way * HZ : LZ + (way + 1) * HZ, :] = (total - high.astype(f32)).astype(bf16)
 
+    def triangular(rows):
+        return lax.dot_general(
+            rows, work[:, R : 2 * R], (((1,), (1,)), ((), ())),
+            preferred_element_type=f32, precision=HIGHEST,
+        )
+
     def sums_over_z(it):
-        for k in range(1, NZ):
+        for k in RING:
             s = lax.rem(z + k, NZ)
             copy(cz.at[it, s], cz.at[it, s], cz_s.at[k], cz_r.at[it, s], at_z(k)).wait_recv()
         total = cz[it, 0]
@@ -154,21 +166,20 @@
         scale[...] = math.sqrt(FF) / jnp.sqrt(cc[it, 0] + cc[it, 1] + norm_eps)
 
     def left_first(it, start):
-        ls[...] = jnp.dot(m[...], f[...], preferred_element_type=f32).astype(bf16)
-        for k in range(1, NY):
+        for k in RING:
             t = lax.rem(y + k, NY)
             start(copy(ls.at[pl.ds(t * LY, LY)], ly.at[it, y], ly_s.at[k], ly_r.at[it, y], at_y(k)))
         ring_step(1)
         total = ls[pl.ds(y * LY, LY), :].astype(f32)
-        for k in range(1, NY):
+        for k in RING:
             s = lax.rem(y + k, NY)
             copy(ly.at[it, s], ly.at[it, s], ly_s.at[k], ly_r.at[it, s], at_y(k)).wait_recv()
             total = total + ly[it, s].astype(f32)
         lz[z] = total.astype(bf16)
-        for k in range(1, NZ):
+        for k in RING:
             start(copy(lz.at[z], lz.at[z], lz_s.at[k], lz_r.at[z], at_z(k)))
         ring_step(2)
-        for k in range(1, NZ):
+        for k in RING:
             s = lax.rem(z + k, NZ)
             copy(lz.at[s], lz.at[s], lz_s.at[k], lz_r.at[s], at_z(k)).wait_recv()
         total = lz[0].astype(f32)
@@ -176,36 +187,36 @@
             total = total + lz[s].astype(f32)
         la[it, pl.ds(y * LY, LY), :] = (total * scale[0:1, :]).astype(bf16)
         mine = la.at[it, pl.ds(y * LY, LY)]
-        for k in range(1, NY):
+        for k in RING:
             start(copy(mine, mine, la_s.at[k], la_r.at[it, y], at_y(k)))
         ring_step(3)
-        for k in range(1, NY):
+        for k in RING:
             s = lax.rem(y + k, NY)
             theirs = la.at[it, pl.ds(s * LY, LY)]
             copy(theirs, theirs, la_s.at[k], la_r.at[it, s], at_y(k)).wait_recv()
 
     def left_later(it, start):
-        both = jnp.dot(ms[...], f[...], preferred_element_type=f32)
+        both = jnp.dot(ms[...], factor(it), preferred_element_type=f32)
         ly[it, y] = (both[0:LZ, :] + both[LZ : 2 * LZ, :]).astype(bf16)
-        for k in range(1, NY):
+        for k in RING:
             start(copy(ly.at[it, y], ly.at[it, y], ly_s.at[k], ly_r.at[it, y], at_y(k)))
         sums_over_z(it - 1)
-        for k in range(1, NY):
+        for k in RING:
             s = lax.rem(y + k, NY)
             copy(ly.at[it, s], ly.at[it, s], ly_s.at[k], ly_r.at[it, s], at_y(k)).wait_recv()
         column_scale(it - 1)
         total = ly[it, 0].astype(f32)
         for s in range(1, NY):
             total = total + ly[it, s].astype(f32)
-        rows = (total * (scale[0:1, :] * (1.0 / NZ))).astype(bf16)
+        rows = (triangular(total) * (scale[0:1, :] * (1.0 / NZ**2))).astype(bf16)
         la[it, pl.ds(z * LZ, LZ), :] = rows
         mine = la.at[it, pl.ds(z * LZ, LZ)]
-        for k in range(1, NZ):
+        for k in RING:
             start(copy(mine, mine, la_s.at[k], la_r.at[it, z], at_z(k)))
         return rows
 
     def wait_left_later(it):
-        for k in range(1, NZ):
+        for k in RING:
             s = lax.rem(z + k, NZ)
             theirs = la.at[it, pl.ds(s * LZ, LZ)]
             copy(theirs, theirs, la_s.at[k], la_r.at[it, s], at_z(k)).wait_recv()
@@ -214,9 +225,10 @@
         columns = pl.ds(pl.multiple_of(half * RC, 128), RC)
         return lax.dot_general(
             block[:, columns], left, (((0,), (0,)), ((), ())), preferred_element_type=f32
-        )
-
-    def iteration(it, first):
+        ).reshape(NZ, RZ, R)
+
+    def iteration(it):
+        first, final = it == 0, it == ITERS - 1
         sends = []
 
         def start(cp):
@@ -232,9 +244,46 @@
 
         def gram_over_x():
             copy(gs, gc.at[it], gc_s, gc_r.at[it], mate).wait_recv()
-            gx[it, x] = gs[...] + gc[it]
-            for k in range(1, NX):
+            gx[it, x] = (gs[...] + gc[it]).astype(bf16)
+            for k in RING_X:
                 start(copy(gx.at[it, x], gx.at[it, x], gx_s.at[k], gx_r.at[it, x], at_x(k)))
+
+        def factorise():
+            for k in RING_X:
+                s = lax.rem(x + k, NX)
+                copy(gx.at[it, s], gx.at[it, s], gx_s.at[k], gx_r.at[it, s], at_x(k)).wait_recv()
+            gram = (gx[it, 0].astype(f32) + gx[it, 1].astype(f32)) + (
+                gx[it, 2].astype(f32) + gx[it, 3].astype(f32)
+            )
+            eye = lax.broadcasted_iota(jnp.int32, (R, R), 0) == lax.broadcasted_iota(
+                jnp.int32, (R, R), 1
+            )
+            ridge = (ridge_scale / R) * jnp.sum(jnp.where(eye, gram, 0.0), keepdims=True)
+            work[:, 0:R] = jnp.where(eye, gram + ridge, gram)
+            work[:, R : 2 * R] = jnp.where(eye, 1.0, 0.0)
+            factor_inverse(work)
+
+        def gather(rows):
+            ra[it + 1, c, z] = rows.astype(bf16)
+            mine = ra.at[it + 1, c, z]
+            for k in RING:
+                start(copy(mine, mine, ra_s.at[k], ra_r.at[it, z], at_z(k)))
+
+        def squares(right):
+            cy[it, y] = jnp.broadcast_to(jnp.sum(right * right, axis=0, keepdims=True), (8, R))
+            for k in RING:
+                start(copy(cy.at[it, y], cy.at[it, y], cy_s.at[k], cy_r.at[it, y], at_y(k)))
+
+        def squares_over_y():
+            for k in RING:
+                s = lax.rem(y + k, NY)
+                copy(cy.at[it, s], cy.at[it, s], cy_s.at[k], cy_r.at[it, s], at_y(k)).wait_recv()
+            total = cy[it, 0]
+            for s in range(1, NY):
+                total = total + cy[it, s]
+            cz[it, z] = total
+            for k in RING:
+                start(copy(cz.at[it, z], cz.at[it, z], cz_s.at[k], cz_r.at[it, z], at_z(k)))
 
         if first:
             left_first(it, start)
@@ -244,88 +293,67 @@
         else:
             rows = left_later(it, start)
             block, rows = ms, jnp.concatenate([rows, rows], 0)
-        rcs[...] = product(block, rows, 1 - c)
+
+        rcs[...] = product(block, rows, 1 - c).astype(bf16)
         to_mate = copy(rcs, rc.at[it], rc_s, rc_r.at[it], mate)
         start(to_mate)
         own = product(block, rows, c)
         if first:
             gram_over_x()
         to_mate.wait_recv()
-        rzs[...] = (own + rc[it]).astype(bf16)
-        for k in range(1, NZ):
+        rzs[...] = (own + rc[it].astype(f32)).astype(bf16)
+        for k in RING:
             t = lax.rem(z + k, NZ)
-            start(copy(rzs.at[pl.ds(t * RZ, RZ)], rz.at[it, z], rz_s.at[k], rz_r.at[it, z], at_z(k)))
-        if not first:
+            start(copy(rzs.at[t], rz.at[it, z], rz_s.at[k], rz_r.at[it, z], at_z(k)))
+        if first:
+            ring_step(5)
+        else:
             wait_left_later(it)
             gram_to_mate()
             gram_over_x()
 
-        for k in range(1, NX):
-            s = lax.rem(x + k, NX)
-            copy(gx.at[it, s], gx.at[it, s], gx_s.at[k], gx_r.at[it, s], at_x(k)).wait_recv()
-        if first:
-            ring_step(5)
-        gram = (gx[it, 0] + gx[it, 1]) + (gx[it, 2] + gx[it, 3])
-        eye = lax.broadcasted_iota(jnp.int32, (R, R), 0) == lax.broadcasted_iota(
-            jnp.int32, (R, R), 1
-        )
-        ridge = (ridge_scale / R) * jnp.sum(jnp.where(eye, gram, 0.0), keepdims=True)
-        work[:, 0:R] = jnp.where(eye, gram + ridge, gram)
-        work[:, R : 2 * R] = jnp.where(eye, 1.0, 0.0)
-        factor_inverse(work)
-
-        total = rzs[pl.ds(z * RZ, RZ), :].astype(f32)
-        for k in range(1, NZ):
+        total = rzs[z].astype(f32)
+        for k in RING:
             s = lax.rem(z + k, NZ)
             copy(rz.at[it, s], rz.at[it, s], rz_s.at[k], rz_r.at[it, s], at_z(k)).wait_recv()
             total = total + rz[it, s].astype(f32)
         rx[it, x] = total.astype(bf16)
-        for k in range(1, NX):
+        for k in RING_X:
             start(copy(rx.at[it, x], rx.at[it, x], rx_s.at[k], rx_r.at[it, x], at_x(k)))
         if first:
             ring_step(6)
-        for k in range(1, NX):
+        if final:
+            factorise()
+        for k in RING_X:
             s = lax.rem(x + k, NX)
             copy(rx.at[it, s], rx.at[it, s], rx_s.at[k], rx_r.at[it, s], at_x(k)).wait_recv()
         total = (rx[it, 0].astype(f32) + rx[it, 1].astype(f32)) + (
             rx[it, 2].astype(f32) + rx[it, 3].astype(f32)
         )
-        right = lax.dot_general(
-            total, work[:, R : 2 * R], (((1,), (1,)), ((), ())),
-            preferred_element_type=f32, precision=HIGHEST,
-        ) * (1.0 / NZ)
-        here = c * RC + z * RZ
-        ra[it, pl.ds(here, RZ), :] = right.astype(bf16)
-        mine = ra.at[it, pl.ds(here, RZ)]
-        for k in range(1, NZ):
-            start(copy(mine, mine, ra_s.at[k], ra_r.at[it, z], at_z(k)))
-        cy[it, y] = jnp.broadcast_to(jnp.sum(right * right, axis=0, keepdims=True), (8, R))
-        for k in range(1, NY):
-            start(copy(cy.at[it, y], cy.at[it, y], cy_s.at[k], cy_r.at[it, y], at_y(k)))
-        start(copy(mine, mine, rm_s.at[0], rm_r.at[it, z], mate))
-        if first:
-            ring_step(7)
-        for k in range(1, NY):
-            s = lax.rem(y + k, NY)
-            copy(cy.at[it, s], cy.at[it, s], cy_s.at[k], cy_r.at[it, s], at_y(k)).wait_recv()
-        total = cy[it, 0]
-        for s in range(1, NY):
-            total = total + cy[it, s]
-        cz[it, z] = total
-        for k in range(1, NZ):
-            start(copy(cz.at[it, z], cz.at[it, z], cz_s.at[k], cz_r.at[it, z], at_z(k)))
-        for k in (1, 7, 2, 6, 3, 5, 4):
+
+        if final:
+            right = triangular(total) * (1.0 / NZ)
+            gather(right)
+            squares(right)
+            squares_over_y()
+        else:
+            gather(total)
+            if first:
+                ring_step(7)
+            factorise()
+            squares(triangular(total) * (1.0 / NZ))
+        for k in RING:
             s = lax.rem(z + k, NZ)
-            theirs = ra.at[it, pl.ds(c * RC + s * RZ, RZ)]
-            copy(theirs, theirs, ra_s.at[k], ra_r.at[it, s], at_z(k)).wait_recv()
-            start(copy(theirs, theirs, rm_s.at[k], rm_r.at[it, s], mate))
+            there = ra.at[it + 1, c, s]
+            copy(there, there, ra_s.at[k], ra_r.at[it, s], at_z(k)).wait_recv()
+        half = ra.at[it + 1, c]
+        start(copy(half, half, rm_s, rm_r.at[it], mate))
+        if not final:
+            squares_over_y()
         if first:
             ring_end()
-        for k in range(NZ):
-            s = lax.rem(z + k, NZ)
-            theirs = ra.at[it, pl.ds((1 - c) * RC + s * RZ, RZ)]
-            copy(theirs, theirs, rm_s.at[k], rm_r.at[it, s], mate).wait_recv()
-        f[...] = ra[it]
+        half = ra.at[it + 1, 1 - c]
+        copy(half, half, rm_s, rm_r.at[it], mate).wait_recv()
         for cp in sends:
             cp.wait_send()
         if first:
@@ -333,19 +361,11 @@
                 for step in range(1, NZ):
                     ring_copy(way, step).wait_send()
 
-    iteration(0, True)
-
-    def again(it, carry):
-        iteration(it, False)
-        return carry
-
-    lax.fori_loop(1, ITERS, again, 0)
+    for it in range(ITERS):
+        iteration(it)
     last = ITERS - 1
-    lr_ref[...] = lax.dot_general(
-        la[last].astype(f32), work[:, R : 2 * R], (((1,), (1,)), ((), ())),
-        preferred_element_type=f32, precision=HIGHEST,
-    ).astype(bf16)
-    rr_ref[...] = f[...]
+    lr_ref[...] = triangular(la[last].astype(f32)).astype(bf16)
+    rr_ref[...] = factor(ITERS)
     sums_over_z(last)
     column_scale(last)
     d_ref[...] = scale[...]
@@ -367,7 +387,6 @@
         out_specs=[vmem] * 3,
         scratch_shapes=[
             pltpu.VMEM((ROWS, COLS), bf16),
-            pltpu.VMEM((COLS, R), bf16),
             pltpu.VMEM((2 * LZ, COLS), bf16),
             pltpu.VMEM((2, NZ - 1, HZ, COLS), bf16),
             pltpu.VMEM((ROWS, R), bf16),
@@ -375,15 +394,15 @@
             pltpu.VMEM((NZ, LY, R), bf16),
             pltpu.VMEM((n, ROWS, R), bf16),
             pltpu.VMEM((n, R, R), f32),
-            pltpu.VMEM((n, NX, R, R), f32),
+            pltpu.VMEM((n, NX, R, R), bf16),
             pltpu.VMEM((R, R), f32),
             pltpu.VMEM((R, 2 * R), f32),
-            pltpu.VMEM((RC, R), f32),
-            pltpu.VMEM((n, RC, R), f32),
-            pltpu.VMEM((RC, R), bf16),
+            pltpu.VMEM((NZ, RZ, R), bf16),
+            pltpu.VMEM((n, NZ, RZ, R), bf16),
+            pltpu.VMEM((NZ, RZ, R), bf16),
             pltpu.VMEM((n, NZ, RZ, R), bf16),
             pltpu.VMEM((n, NX, RZ, R), bf16),
-            pltpu.VMEM((n, COLS, R), bf16),
+            pltpu.VMEM((n + 1, 2, NZ, RZ, R), bf16),
             pltpu.VMEM((n, NY, 8, R), f32),
             pltpu.VMEM((n, NZ, 8, R), f32),
             pltpu.VMEM((n, 2, 8, R), f32),
@@ -399,7 +418,7 @@
             dma((NZ,)), dma((n, NZ)),
             dma((NX,)), dma((n, NX)),
             dma((NZ,)), dma((n, NZ)),
-            dma((NZ,)), dma((n, NZ)),
+            dma(()), dma((n,)),
             dma((NY,)), dma((n, NY)),
             dma((NZ,)), dma((n, NZ)),
             dma(()), dma((n,)),
@@ -410,7 +429,7 @@
         cost_estimate=pl.CostEstimate(
             flops=12 * ROWS * COLS * R, bytes_accessed=2 * ROWS * COLS, transcendentals=0
         ),
-    )(block, q)
+    )(block, q.reshape(2, NZ, RZ, R))
 
 
 def finish_kernel(m, left, right, scale, m_out, u_out, q_out):
@@ -426,7 +445,7 @@
 
 
 def finish(block, left, right, scale):
-    steps = 4
+    steps = 2
     rows = ROWS // steps
     return pl.pallas_call(
         finish_kernel,

time: 143 us -> 129 us (0.902)
  Pallas kernels: 142 us -> 128 us
    pallas_call x1, Pallas kernels: 137 us -> 125 us  [iterate(): pl.pallas_call(iterate_kernel, out_shape=[jax.ShapeDtypeStruct((ROWS, R),...]
where the time goes in v4:
time: 129 us
  Pallas kernels  128 us (99%)
    pallas_call x1, Pallas kernels, iterate(): pl.pallas_call(iterate_kernel, out_shape=[jax.ShapeDtypeStruct((ROWS, R),...  125 us
    pallas_call x1, Pallas kernels, finish(): pl.pallas_call(finish_kernel, grid=(steps,), out_shape=[jax.ShapeDtypeStr...  3.4 us

profile of v4, /device:TPU:1, one launch (start us, length us, event | category | flops | bytes accessed | tf_op | source)
XLA Modules:
  0.0 128.9 jit_solution(2979205652856146545)
XLA Ops:
  0.6 124.8 %shard_map.49 = (bf16[512,128]{1,0:T(8,128)(2,1)}, bf16[1792,128]{1,0:T(8,128)(2,1)}, f32[8,128]{1,0:T(8,128)}) custom-call(bf16[512,1792]{1,0:T(8,128)(2,1)} %bitcast.3, bf16[2,8,112,128]{3,2,1,0:T(8,128)(2,1)} %bitcast.6), custom_call_target="tpu_custom_call" | custom-call | flops 1409286144 | bytes 1835008 | tf_op jit(solution)/shard_map/pallas_call | solution.py:379
  125.5 3.4 %shard_map.50 = (bf16[512,1792]{1,0:T(8,128)(2,1)}, f32[512,128]{1,0:T(8,128)}, bf16[1792,128]{1,0:T(8,128)(2,1)}) custom-call(bf16[512,1792]{1,0:T(8,128)(2,1)} %bitcast.4, bf16[512,128]{1,0:T(8,128)(2,1)} %get-tuple-element.9.left, bf16[1792,128]{1,0:T(8,128)(2,1)} %get-tuple-element.10.right, f32[8,128]{1,0:T(8,128)} %get-tuple-element.11.scale), custom_call_target="tpu_custom_call" | custom-call | flops 234881024 | bytes 3670016 | tf_op jit(solution)/shard_map/pallas_call | solution.py:450

commit v5 on v4

--- a/solution.py
+++ b/solution.py
@@ -17,7 +17,7 @@
 COLS = 1792
 LY = ROWS // NY
 LZ = ROWS // NZ
-HZ = LZ // 2
+LINKS = (4, 3)
 RC = COLS // 2
 RZ = RC // NZ
 RING = (4, 3, 5, 2, 6, 1, 7)
@@ -117,33 +117,34 @@
     ls[...] = jnp.dot(m[...], factor(0), preferred_element_type=f32).astype(bf16)
     pl.semaphore_wait(barrier, NY + NZ + NX - 2)
 
-    def chunk(way, j):
-        return pl.ds(pl.multiple_of(lax.rem(j + 2 * NZ, NZ) * LZ + way * HZ, HZ), HZ)
+    def chunk(j):
+        return pl.ds(pl.multiple_of(lax.rem(j + 2 * NZ, NZ) * LZ, LZ), LZ)
+
+    def ring_chunk(way, step):
+        return chunk(z + 5 - step if way == 0 else z - 4 + step)
 
     def ring_copy(way, step):
-        step_to = 1 if way == 0 else NZ - 1
-        if step == 1:
-            src = m.at[chunk(way, z - 1 if way == 0 else z + 1)]
-        else:
-            src = ring.at[way, step - 2]
+        src = m.at[ring_chunk(way, 1)] if step == 1 else ring.at[way, step - 2]
         return copy(src, ring.at[way, step - 1], ring_s.at[way, step - 1],
-                    ring_r.at[way, step - 1], at_z(step_to))
+                    ring_r.at[way, step - 1], at_z(1 if way == 0 else NZ - 1))
 
     def ring_step(step):
         for way in range(2):
-            if step > 1:
-                ring_copy(way, step - 1).wait_recv()
-                own = m[chunk(way, z - step if way == 0 else z + step), :].astype(f32)
-                ring[way, step - 2] = (ring[way, step - 2].astype(f32) + own).astype(bf16)
-            ring_copy(way, step).start()
+            if step <= LINKS[way]:
+                if step > 1:
+                    ring_copy(way, step - 1).wait_recv()
+                    own = m[ring_chunk(way, step), :].astype(f32)
+                    ring[way, step - 2] = (ring[way, step - 2].astype(f32) + own).astype(bf16)
+                ring_copy(way, step).start()
 
     def ring_end():
+        total = m[chunk(z), :].astype(f32)
         for way in range(2):
-            ring_copy(way, NZ - 1).wait_recv()
-            total = ring[way, NZ - 2].astype(f32) + m[chunk(way, z), :].astype(f32)
-            high = total.astype(bf16)
-            ms[way * HZ : (way + 1) * HZ, :] = high
-            ms[LZ + way * HZ : LZ + (way + 1) * HZ, :] = (total - high.astype(f32)).astype(bf16)
+            ring_copy(way, LINKS[way]).wait_recv()
+            total = total + ring[way, LINKS[way] - 1].astype(f32)
+        high = total.astype(bf16)
+        ms[0:LZ, :] = high
+        ms[LZ : 2 * LZ, :] = (total - high.astype(f32)).astype(bf16)
 
     def triangular(rows):
         return lax.dot_general(
@@ -178,7 +179,6 @@
         lz[z] = total.astype(bf16)
         for k in RING:
             start(copy(lz.at[z], lz.at[z], lz_s.at[k], lz_r.at[z], at_z(k)))
-        ring_step(2)
         for k in RING:
             s = lax.rem(z + k, NZ)
             copy(lz.at[s], lz.at[s], lz_s.at[k], lz_r.at[s], at_z(k)).wait_recv()
@@ -189,7 +189,7 @@
         mine = la.at[it, pl.ds(y * LY, LY)]
         for k in RING:
             start(copy(mine, mine, la_s.at[k], la_r.at[it, y], at_y(k)))
-        ring_step(3)
+        ring_step(2)
         for k in RING:
             s = lax.rem(y + k, NY)
             theirs = la.at[it, pl.ds(s * LY, LY)]
@@ -287,7 +287,6 @@
 
         if first:
             left_first(it, start)
-            ring_step(4)
             gram_to_mate()
             block, rows = m, la[it]
         else:
@@ -306,7 +305,7 @@
             t = lax.rem(z + k, NZ)
             start(copy(rzs.at[t], rz.at[it, z], rz_s.at[k], rz_r.at[it, z], at_z(k)))
         if first:
-            ring_step(5)
+            ring_step(3)
         else:
             wait_left_later(it)
             gram_to_mate()
@@ -320,8 +319,6 @@
         rx[it, x] = total.astype(bf16)
         for k in RING_X:
             start(copy(rx.at[it, x], rx.at[it, x], rx_s.at[k], rx_r.at[it, x], at_x(k)))
-        if first:
-            ring_step(6)
         if final:
             factorise()
         for k in RING_X:
@@ -339,7 +336,7 @@
         else:
             gather(total)
             if first:
-                ring_step(7)
+                ring_step(4)
             factorise()
             squares(triangular(total) * (1.0 / NZ))
         for k in RING:
@@ -358,7 +355,7 @@
             cp.wait_send()
         if first:
             for way in range(2):
-                for step in range(1, NZ):
+                for step in range(1, LINKS[way] + 1):
                     ring_copy(way, step).wait_send()
 
     for it in range(ITERS):
@@ -388,7 +385,7 @@
         scratch_shapes=[
             pltpu.VMEM((ROWS, COLS), bf16),
             pltpu.VMEM((2 * LZ, COLS), bf16),
-            pltpu.VMEM((2, NZ - 1, HZ, COLS), bf16),
+            pltpu.VMEM((2, 4, LZ, COLS), bf16),
             pltpu.VMEM((ROWS, R), bf16),
             pltpu.VMEM((n, NY, LY, R), bf16),
             pltpu.VMEM((NZ, LY, R), bf16),
@@ -408,7 +405,7 @@
             pltpu.VMEM((n, 2, 8, R), f32),
             pltpu.VMEM((8, R), f32),
             dma(()), dma(()),
-            dma((2, NZ - 1)), dma((2, NZ - 1)),
+            dma((2, 4)), dma((2, 4)),
             dma((NY,)), dma((n, NY)),
             dma((NZ,)), dma((NZ,)),
             dma((NY,)), dma((n, NY)),

time: 129 us -> 123 us (0.953)
  Pallas kernels: 128 us -> 122 us
    pallas_call x1, Pallas kernels: 125 us -> 118 us  [iterate(): pl.pallas_call(iterate_kernel, out_shape=[jax.ShapeDtypeStruct((ROWS, R),...]
where the time goes in v5:
time: 123 us; the launch traced here: 122 us
  Pallas kernels  122 us (99%)
    pallas_call x1, Pallas kernels, iterate(): pl.pallas_call(iterate_kernel, out_shape=[jax.ShapeDtypeStruct((ROWS, R),...  118 us
    pallas_call x1, Pallas kernels, finish(): pl.pallas_call(finish_kernel, grid=(steps,), out_shape=[jax.ShapeDtypeStr...  3.38 us

profile of v5, /device:TPU:1, one launch (start us, length us, event | category | flops | bytes accessed | tf_op | source)
XLA Modules:
  0.0 122.4 jit_solution(6782340150728857142)
XLA Ops:
  0.6 118.3 %shard_map.49 = (bf16[512,128]{1,0:T(8,128)(2,1)}, bf16[1792,128]{1,0:T(8,128)(2,1)}, f32[8,128]{1,0:T(8,128)}) custom-call(bf16[512,1792]{1,0:T(8,128)(2,1)} %bitcast.3, bf16[2,8,112,128]{3,2,1,0:T(8,128)(2,1)} %bitcast.6), custom_call_target="tpu_custom_call" | custom-call | flops 1409286144 | bytes 1835008 | tf_op jit(solution)/shard_map/pallas_call | solution.py:376
  119.0 3.4 %shard_map.50 = (bf16[512,1792]{1,0:T(8,128)(2,1)}, f32[512,128]{1,0:T(8,128)}, bf16[1792,128]{1,0:T(8,128)(2,1)}) custom-call(bf16[512,1792]{1,0:T(8,128)(2,1)} %bitcast.4, bf16[512,128]{1,0:T(8,128)(2,1)} %get-tuple-element.9.left, bf16[1792,128]{1,0:T(8,128)(2,1)} %get-tuple-element.10.right, f32[8,128]{1,0:T(8,128)} %get-tuple-element.11.scale), custom_call_target="tpu_custom_call" | custom-call | flops 234881024 | bytes 3670016 | tf_op jit(solution)/shard_map/pallas_call | solution.py:447

commit v6 on v5

v6 whole, which is shorter than its diff:
```python
import functools
import math

import jax
import jax.numpy as jnp
from jax import lax
from jax.experimental import pallas as pl
from jax.experimental.pallas import tpu as pltpu
from jax.sharding import PartitionSpec as P

D = 4096
FF = 14336
R = 128
ITERS = 3
NY, NZ, NX = 8, 8, 4
ROWS = 512
COLS = 1792
LY = ROWS // NY
HALF = 128
CZ = 2 * HALF
PAD = NZ * CZ
LINKS = (4, 3)
RING = (4, 3, 5, 2, 6, 1, 7)
RING_X = (2, 1, 3)
PLACES = "ABCD"

ridge_scale = 1e-06
norm_eps = 1e-06
momentum_decay = 0.95

MESH = pl.DeviceIdType.MESH
f32, bf16 = jnp.float32, jnp.bfloat16
HIGHEST = lax.Precision.HIGHEST


def split3(w):
    high = w.astype(bf16).astype(f32)
    rest = w - high
    mid = rest.astype(bf16).astype(f32)
    return high, mid, rest - mid


def factor_inverse(work):
    size = 16
    sub = lax.broadcasted_iota(jnp.int32, (size, R), 0)
    lane = lax.broadcasted_iota(jnp.int32, (size, R), 1)
    for first in range(0, R, size):
        left, right = work[first : first + size, 0:R], work[first : first + size, R : 2 * R]
        cols = [
            jnp.broadcast_to(left[:, first + k : first + k + 1], (size, R)) for k in range(size)
        ]
        scale = jnp.zeros((size, R), f32)
        for j in range(size):
            pivot = jnp.broadcast_to(cols[j][j : j + 1, :], (size, R))
            scale = jnp.where(sub == j, lax.rsqrt(pivot), scale)
            if j < size - 1:
                ratio = jnp.where(sub > j, cols[j], 0.0) * (1.0 / pivot)
                for k in range(j + 1, size):
                    cols[k] = cols[k] - ratio * cols[k][j : j + 1, :]
                left = left - ratio * left[j : j + 1, :]
                right = right - ratio * right[j : j + 1, :]
        left = jnp.where(lane >= first, left * scale, 0.0)
        right = right * scale
        work[first : first + size, 0:R] = left
        work[first : first + size, R : 2 * R] = right
        below = first + size
        if below < R:
            ph, pm, pw = split3(jnp.concatenate([left, right], 1))
            wh, wm, ww = split3(jnp.where(lane >= below, left, 0.0))
            a = jnp.concatenate([wh, wh, wm, wm, wh, ww], 0).astype(bf16)
            b = jnp.concatenate([ph, pm, ph, pm, pw, ph], 0).astype(bf16)
            update = lax.dot_general(a, b, (((0,), (0,)), ((), ())), preferred_element_type=f32)
            work[below:R, :] = work[below:R, :] - update[below:R, :]


def iterate_kernel(
    m_hbm, q_hbm, lr_ref, rr_ref, d_ref,
    m, q, ms, ring, ls, ly, lz, la, gc, gx, gs, work, rcs, rc, rzs, rz, r2, r2s, r2c, rx, ra, rf,
    cy, cz, cc, m_sem, q_sem, ring_s, ring_r, ly_s, ly_r, lz_s, lz_r, la_s, la_r, gc_s, gc_r,
    gx_s, gx_r, rc_s, rc_r, rz_s, rz_r, rx_s, rx_r, ra_s, ra_r, rf_s, rf_r, rm_s, rm_r,
    cy_s, cy_r, cz_s, cz_r, cc_s, cc_r,
):
    z, fs, y = lax.axis_index("replica"), lax.axis_index("fsdp"), lax.axis_index("tensor")
    x, c = fs // 2, lax.rem(fs, 2)
    mate = {"fsdp": x * 2 + 1 - c}

    def at_y(k):
        return {"tensor": lax.rem(y + k, NY)}

    def at_z(k):
        return {"replica": lax.rem(z + k, NZ)}

    def at_x(k):
        return {"fsdp": lax.rem(x + k, NX) * 2 + c}

    def copy(src, dst, send, recv, to):
        return pltpu.make_async_remote_copy(
            src_ref=src, dst_ref=dst, send_sem=send, recv_sem=recv, device_id=to, device_id_type=MESH
        )

    barrier = pltpu.get_barrier_semaphore()
    for k in RING:
        pl.semaphore_signal(barrier, inc=1, device_id=at_y(k), device_id_type=MESH)
        pl.semaphore_signal(barrier, inc=1, device_id=at_z(k), device_id_type=MESH)
    for k in RING_X:
        pl.semaphore_signal(barrier, inc=1, device_id=at_x(k), device_id_type=MESH)
    pl.semaphore_signal(barrier, inc=1, device_id=mate, device_id_type=MESH)
    load_m = pltpu.make_async_copy(m_hbm, m.at[:, pl.ds(0, COLS)], m_sem)
    load_m.start()
    load_q = pltpu.make_async_copy(q_hbm, q, q_sem)
    load_q.start()
    m[:, COLS:PAD] = jnp.zeros((ROWS, PAD - COLS), bf16)
    load_q.wait()
    load_m.wait()
    ls[0] = jnp.dot(m[:, 0:COLS], q[...], preferred_element_type=f32).astype(bf16)
    pl.semaphore_wait(barrier, NY + NZ + NX - 2)

    def chunk(j):
        return pl.ds(pl.multiple_of(lax.rem(j + 2 * NZ, NZ) * CZ, CZ), CZ)

    def ring_chunk(way, step):
        return chunk(z + 5 - step if way == 0 else z - 4 + step)

    def ring_copy(way, step):
        src = m.at[:, ring_chunk(way, 1)] if step == 1 else ring.at[way, step - 2]
        return copy(src, ring.at[way, step - 1], ring_s.at[way, step - 1],
                    ring_r.at[way, step - 1], at_z(1 if way == 0 else NZ - 1))

    def ring_step(step):
        for way in range(2):
            if step <= LINKS[way]:
                if step > 1:
                    ring_copy(way, step - 1).wait_recv()
                    own = m[:, ring_chunk(way, step)].astype(f32)
                    ring[way, step - 2] = (ring[way, step - 2].astype(f32) + own).astype(bf16)
                ring_copy(way, step).start()

    def ring_end():
        total = m[:, chunk(z)].astype(f32)
        for way in range(2):
            ring_copy(way, LINKS[way]).wait_recv()
            total = total + ring[way, LINKS[way] - 1].astype(f32)
        high = total.astype(bf16)
        ms[:, 0:CZ] = high
        ms[:, CZ : 2 * CZ] = (total - high.astype(f32)).astype(bf16)

    sends = []

    def start(cp):
        cp.start()
        sends.append(cp)

    def wait_sends():
        for cp in sends:
            cp.wait_send()
        sends.clear()

    def triangular(rows):
        return lax.dot_general(
            rows, work[:, R : 2 * R], (((1,), (1,)), ((), ())),
            preferred_element_type=f32, precision=HIGHEST,
        )

    def squares(it, right):
        cy[it, y] = jnp.broadcast_to(jnp.sum(right * right, axis=0, keepdims=True), (8, R))
        for k in RING:
            start(copy(cy.at[it, y], cy.at[it, y], cy_s.at[k], cy_r.at[it, y], at_y(k)))

    def squares_over_y(it):
        for k in RING:
            s = lax.rem(y + k, NY)
            copy(cy.at[it, s], cy.at[it, s], cy_s.at[k], cy_r.at[it, s], at_y(k)).wait_recv()
        total = cy[it, 0]
        for s in range(1, NY):
            total = total + cy[it, s]
        cz[it, z] = total
        for k in RING:
            start(copy(cz.at[it, z], cz.at[it, z], cz_s.at[k], cz_r.at[it, z], at_z(k)))

    def squares_over_z(it):
        for k in RING:
            s = lax.rem(z + k, NZ)
            copy(cz.at[it, s], cz.at[it, s], cz_s.at[k], cz_r.at[it, s], at_z(k)).wait_recv()
        total = cz[it, 0]
        for s in range(1, NZ):
            total = total + cz[it, s]
        cc[it, 0] = total
        start(copy(cc.at[it, 0], cc.at[it, 1], cc_s, cc_r.at[it], mate))

    def column_scale(it):
        copy(cc.at[it, 0], cc.at[it, 1], cc_s, cc_r.at[it], mate).wait_recv()
        return math.sqrt(FF) / jnp.sqrt(cc[it, 0] + cc[it, 1] + norm_eps)

    def factorise(it):
        for k in RING_X:
            s = lax.rem(x + k, NX)
            copy(gx.at[it, s], gx.at[it, s], gx_s.at[k], gx_r.at[it, s], at_x(k)).wait_recv()
        gram = (gx[it, 0].astype(f32) + gx[it, 1].astype(f32)) + (
            gx[it, 2].astype(f32) + gx[it, 3].astype(f32)
        )
        if it > 0:
            scale = jnp.broadcast_to(column_scale(it - 1)[0:1, :], (R, R))
            gram = gram * scale * scale.T
        eye = lax.broadcasted_iota(jnp.int32, (R, R), 0) == lax.broadcasted_iota(
            jnp.int32, (R, R), 1
        )
        ridge = (ridge_scale / R) * jnp.sum(jnp.where(eye, gram, 0.0), keepdims=True)
        work[:, 0:R] = jnp.where(eye, gram + ridge, gram)
        work[:, R : 2 * R] = jnp.where(eye, 1.0, 0.0)
        factor_inverse(work)
        if it > 0:
            work[:, R : 2 * R] = work[:, R : 2 * R] * scale

    def right_total(it):
        return (rx[it, 0].astype(f32) + rx[it, 1].astype(f32)) + (
            rx[it, 2].astype(f32) + rx[it, 3].astype(f32)
        )

    def left_factor(it):
        if it > 0:
            there = ra.at[it - 1, 1 - c]
            copy(there, there, ra_s, ra_r.at[it - 1], mate).wait_recv()
            rows = ra[it - 1].reshape(CZ, R)
            if it == 1:
                ring_end()
            ls[it] = jnp.dot(
                ms[...], jnp.concatenate([rows, rows], 0), preferred_element_type=f32
            ).astype(bf16)
        for k in RING:
            t = lax.rem(y + k, NY)
            start(copy(ls.at[it, pl.ds(t * LY, LY)], ly.at[it, y], ly_s.at[k], ly_r.at[it, y], at_y(k)))
        if it > 0:
            factorise(it - 1)
            squares(it - 1, triangular(right_total(it - 1)) * (1.0 / NZ))
        ring_at(it, "A")
        total = ls[it, pl.ds(y * LY, LY), :].astype(f32)
        for k in RING:
            s = lax.rem(y + k, NY)
            copy(ly.at[it, s], ly.at[it, s], ly_s.at[k], ly_r.at[it, s], at_y(k)).wait_recv()
            total = total + ly[it, s].astype(f32)
        lz[it, z] = total.astype(bf16)
        for k in RING:
            start(copy(lz.at[it, z], lz.at[it, z], lz_s.at[k], lz_r.at[it, z], at_z(k)))
        if it > 0:
            squares_over_y(it - 1)
        ring_at(it, "B")
        for k in RING:
            s = lax.rem(z + k, NZ)
            copy(lz.at[it, s], lz.at[it, s], lz_s.at[k], lz_r.at[it, s], at_z(k)).wait_recv()
        total = lz[it, 0].astype(f32)
        for s in range(1, NZ):
            total = total + lz[it, s].astype(f32)
        total = total * (1.0 / NZ) if it == 0 else triangular(total) * (1.0 / NZ**2)
        la[it, pl.ds(y * LY, LY), :] = total.astype(bf16)
        mine = la.at[it, pl.ds(y * LY, LY)]
        for k in RING:
            start(copy(mine, mine, la_s.at[k], la_r.at[it, y], at_y(k)))
        if it > 0:
            squares_over_z(it - 1)
        ring_at(it, "C")
        for k in RING:
            s = lax.rem(y + k, NY)
            theirs = la.at[it, pl.ds(s * LY, LY)]
            copy(theirs, theirs, la_s.at[k], la_r.at[it, s], at_y(k)).wait_recv()

    def ring_at(it, point):
        if it == 0 and point in PLACES:
            ring_step(PLACES.index(point) + 1)

    def right_factor(it):
        left = la[it]
        gs[it] = lax.dot_general(left, left, (((0,), (0,)), ((), ())), preferred_element_type=f32)
        start(copy(gs.at[it], gc.at[it], gc_s, gc_r.at[it], mate))
        if it == 0:
            rcs[...] = (
                lax.dot_general(m[...], left, (((0,), (0,)), ((), ())), preferred_element_type=f32)
                .astype(bf16)
                .reshape(NZ, 2, HALF, R)
            )
            to_mate = copy(rcs.at[:, 1 - c], rc, rc_s, rc_r.at[it], mate)
        else:
            both = lax.dot_general(ms[...], left, (((0,), (0,)), ((), ())), preferred_element_type=f32)
            both = (both[0:CZ, :] + both[CZ : 2 * CZ, :]).reshape(2, HALF, R)
            r2[...] = both
            r2s[it] = both.astype(bf16)
            to_mate = copy(r2s.at[it, 1 - c], r2c.at[it], rc_s, rc_r.at[it], mate)
        start(to_mate)
        copy(gs.at[it], gc.at[it], gc_s, gc_r.at[it], mate).wait_recv()
        gx[it, x] = (gs[it] + gc[it]).astype(bf16)
        for k in RING_X:
            start(copy(gx.at[it, x], gx.at[it, x], gx_s.at[k], gx_r.at[it, x], at_x(k)))
        to_mate.wait_recv()
        if it == 0:
            rzs[...] = (rcs[:, c].astype(f32) + rc[...].astype(f32)).astype(bf16)
            for k in RING:
                t = lax.rem(z + k, NZ)
                start(copy(rzs.at[t], rz.at[z], rz_s.at[k], rz_r.at[z], at_z(k)))
            ring_at(it, "D")
            total = rzs[z].astype(f32)
            for k in RING:
                s = lax.rem(z + k, NZ)
                copy(rz.at[s], rz.at[s], rz_s.at[k], rz_r.at[s], at_z(k)).wait_recv()
                total = total + rz[s].astype(f32)
        else:
            total = r2[c] + r2c[it].astype(f32)
        rx[it, x] = total.astype(bf16)
        for k in RING_X:
            start(copy(rx.at[it, x], rx.at[it, x], rx_s.at[k], rx_r.at[it, x], at_x(k)))
        ring_at(it, "E")
        if it == ITERS - 1:
            factorise(it)
        for k in RING_X:
            s = lax.rem(x + k, NX)
            copy(rx.at[it, s], rx.at[it, s], rx_s.at[k], rx_r.at[it, s], at_x(k)).wait_recv()

    last = ITERS - 1
    for it in range(ITERS):
        left_factor(it)
        right_factor(it)
        if it < last:
            wait_sends()
            ra[it, c] = right_total(it).astype(bf16)
            start(copy(ra.at[it, c], ra.at[it, c], ra_s, ra_r.at[it], mate))

    right = triangular(right_total(last)) * (1.0 / NZ)
    squares(last, right)
    rf[z, c] = right.astype(bf16)
    mine = rf.at[z, c]
    for k in RING:
        start(copy(mine, mine, rf_s.at[k], rf_r.at[z], at_z(k)))
    lr_ref[...] = triangular(la[last].astype(f32)).astype(bf16)
    squares_over_y(last)
    for k in RING:
        s = lax.rem(z + k, NZ)
        there = rf.at[s, c]
        copy(there, there, rf_s.at[k], rf_r.at[s], at_z(k)).wait_recv()
    half = rf.at[:, c]
    start(copy(half, half, rm_s, rm_r, mate))
    squares_over_z(last)
    half = rf.at[:, 1 - c]
    copy(half, half, rm_s, rm_r, mate).wait_recv()
    rr_ref[...] = rf[...].reshape(PAD, R)[0:COLS, :]
    d_ref[...] = column_scale(last)
    wait_sends()
    for way in range(2):
        for step in range(1, LINKS[way] + 1):
            ring_copy(way, step).wait_send()


def iterate(block, q):
    vmem = pl.BlockSpec(memory_space=pltpu.VMEM)
    hbm = pl.BlockSpec(memory_space=pltpu.HBM)
    dma = pltpu.SemaphoreType.DMA
    n = ITERS
    return pl.pallas_call(
        iterate_kernel,
        out_shape=[
            jax.ShapeDtypeStruct((ROWS, R), bf16),
            jax.ShapeDtypeStruct((COLS, R), bf16),
            jax.ShapeDtypeStruct((8, R), f32),
        ],
        in_specs=[hbm, hbm],
        out_specs=[vmem] * 3,
        scratch_shapes=[
            pltpu.VMEM((ROWS, PAD), bf16),
            pltpu.VMEM((COLS, R), bf16),
            pltpu.VMEM((ROWS, 2 * CZ), bf16),
            pltpu.VMEM((2, 4, ROWS, CZ), bf16),
            pltpu.VMEM((n, ROWS, R), bf16),
            pltpu.VMEM((n, NY, LY, R), bf16),
            pltpu.VMEM((n, NZ, LY, R), bf16),
            pltpu.VMEM((n, ROWS, R), bf16),
            pltpu.VMEM((n, R, R), f32),
            pltpu.VMEM((n, NX, R, R), bf16),
            pltpu.VMEM((n, R, R), f32),
            pltpu.VMEM((R, 2 * R), f32),
            pltpu.VMEM((NZ, 2, HALF, R), bf16),
            pltpu.VMEM((NZ, HALF, R), bf16),
            pltpu.VMEM((NZ, HALF, R), bf16),
            pltpu.VMEM((NZ, HALF, R), bf16),
            pltpu.VMEM((2, HALF, R), f32),
            pltpu.VMEM((n, 2, HALF, R), bf16),
            pltpu.VMEM((n, HALF, R), bf16),
            pltpu.VMEM((n, NX, HALF, R), bf16),
            pltpu.VMEM((n, 2, HALF, R), bf16),
            pltpu.VMEM((NZ, 2, HALF, R), bf16),
            pltpu.VMEM((n, NY, 8, R), f32),
            pltpu.VMEM((n, NZ, 8, R), f32),
            pltpu.VMEM((n, 2, 8, R), f32),
            dma(()), dma(()),
            dma((2, 4)), dma((2, 4)),
            dma((NY,)), dma((n, NY)),
            dma((NZ,)), dma((n, NZ)),
            dma((NY,)), dma((n, NY)),
            dma(()), dma((n,)),
            dma((NX,)), dma((n, NX)),
            dma(()), dma((n,)),
            dma((NZ,)), dma((NZ,)),
            dma((NX,)), dma((n, NX)),
            dma(()), dma((n,)),
            dma((NZ,)), dma((NZ,)),
            dma(()), dma(()),
            dma((NY,)), dma((n, NY)),
            dma((NZ,)), dma((n, NZ)),
            dma(()), dma((n,)),
        ],
        compiler_params=pltpu.CompilerParams(
            collective_id=0, has_side_effects=True, vmem_limit_bytes=56 << 20
        ),
        cost_estimate=pl.CostEstimate(
            flops=12 * ROWS * COLS * R, bytes_accessed=2 * ROWS * COLS, transcendentals=0
        ),
    )(block, q)


def finish_kernel(m, left, right, scale, m_out, u_out, q_out):
    correction = lax.dot_general(
        left[...], right[...], (((1,), (1,)), ((), ())), preferred_element_type=f32
    )
    m_out[...] = (m[...].astype(f32) - (1.0 - momentum_decay) * correction).astype(bf16)
    u_out[...] = math.sqrt(D) * left[...].astype(f32)

    @pl.when(pl.program_id(0) == 0)
    def _():
        q_out[...] = (right[...].astype(f32) * scale[0:1, :]).astype(bf16)


def finish(block, left, right, scale):
    steps = 2
    rows = ROWS // steps
    return pl.pallas_call(
        finish_kernel,
        grid=(steps,),
        out_shape=[
            jax.ShapeDtypeStruct((ROWS, COLS), bf16),
            jax.ShapeDtypeStruct((ROWS, R), f32),
            jax.ShapeDtypeStruct((COLS, R), bf16),
        ],
        in_specs=[
            pl.BlockSpec((rows, COLS), lambda i: (i, 0)),
            pl.BlockSpec((rows, R), lambda i: (i, 0)),
            pl.BlockSpec((COLS, R), lambda i: (0, 0)),
            pl.BlockSpec((8, R), lambda i: (0, 0)),
        ],
        out_specs=[
            pl.BlockSpec((rows, COLS), lambda i: (i, 0)),
            pl.BlockSpec((rows, R), lambda i: (i, 0)),
            pl.BlockSpec((COLS, R), lambda i: (0, 0)),
        ],
        compiler_params=pltpu.CompilerParams(vmem_limit_bytes=56 << 20),
        cost_estimate=pl.CostEstimate(
            flops=2 * ROWS * COLS * R, bytes_accessed=4 * ROWS * COLS, transcendentals=0
        ),
    )(block, left, right, scale)


def shards(momentum, q_prev):
    block = momentum[0]
    left, right, scale = iterate(block, q_prev)
    momentum_next, update_left, q_next = finish(block, left, right, scale)
    return momentum_next[None], update_left, q_next


def solution(mesh):
    in_specs = (P("replica", "fsdp", "tensor"), P("tensor", None))
    out_specs = (P("replica", "fsdp", "tensor"), P("fsdp", None), P("tensor", None))
    return jax.shard_map(shards, mesh=mesh, in_specs=in_specs, out_specs=out_specs, check_vma=False)
```

time: 123 us -> 119 us (0.967)
  Pallas kernels: 122 us -> 118 us
    pallas_call x1, Pallas kernels: 118 us -> 114 us  [iterate(): pl.pallas_call(iterate_kernel, out_shape=[jax.ShapeDtypeStruct((ROWS, R),...]
where the time goes in v6:
time: 119 us; the launch traced here: 118 us
  Pallas kernels  118 us (99%)
    pallas_call x1, Pallas kernels, iterate(): pl.pallas_call(iterate_kernel, out_shape=[jax.ShapeDtypeStruct((ROWS, R),...  114 us
    pallas_call x1, Pallas kernels, finish(): pl.pallas_call(finish_kernel, grid=(steps,), out_shape=[jax.ShapeDtypeStr...  3.38 us

profile of v6, /device:TPU:1, one launch (start us, length us, event | category | flops | bytes accessed | tf_op | source)
XLA Modules:
  0.0 118.5 jit_solution(2454412230456889201)
XLA Ops:
  0.6 114.4 %shard_map.49 = (bf16[512,128]{1,0:T(8,128)(2,1)}, bf16[1792,128]{1,0:T(8,128)(2,1)}, f32[8,128]{1,0:T(8,128)}) custom-call(bf16[512,1792]{1,0:T(8,128)(2,1)} %bitcast.2, bf16[1792,128]{1,0:T(8,128)(2,1)} %q_hbm.1), custom_call_target="tpu_custom_call" | custom-call | flops 1409286144 | bytes 1835008 | tf_op jit(solution)/shard_map/pallas_call | solution.py:355
  115.1 3.4 %shard_map.50 = (bf16[512,1792]{1,0:T(8,128)(2,1)}, f32[512,128]{1,0:T(8,128)}, bf16[1792,128]{1,0:T(8,128)(2,1)}) custom-call(bf16[512,1792]{1,0:T(8,128)(2,1)} %bitcast.3, bf16[512,128]{1,0:T(8,128)(2,1)} %get-tuple-element.9.left, bf16[1792,128]{1,0:T(8,128)(2,1)} %get-tuple-element.10.right, f32[8,128]{1,0:T(8,128)} %get-tuple-element.11.scale), custom_call_target="tpu_custom_call" | custom-call | flops 234881024 | bytes 3670016 | tf_op jit(solution)/shard_map/pallas_call | solution.py:431

commit v7 on v6

--- a/solution.py
+++ b/solution.py
@@ -19,6 +19,8 @@
 HALF = 128
 CZ = 2 * HALF
 PAD = NZ * CZ
+LS = LY // 2
+LOADS = 4
 LINKS = (4, 3)
 RING = (4, 3, 5, 2, 6, 1, 7)
 RING_X = (2, 1, 3)
@@ -75,10 +77,10 @@
 
 def iterate_kernel(
     m_hbm, q_hbm, lr_ref, rr_ref, d_ref,
-    m, q, ms, ring, ls, ly, lz, la, gc, gx, gs, work, rcs, rc, rzs, rz, r2, r2s, r2c, rx, ra, rf,
-    cy, cz, cc, m_sem, q_sem, ring_s, ring_r, ly_s, ly_r, lz_s, lz_r, la_s, la_r, gc_s, gc_r,
+    m, q, ms, ring, ls, ly, lz, p1, p2, la, gc, gx, gs, work, rcs, rc, ro, rzs, rz, r2, r2s, r2c, rx, ra, rf, rfm,
+    cy, cz, column_sq, m_sem, q_sem, ring_s, ring_r, ly_s, ly_r, lz_s, lz_r, p1_s, p1_r, p2_s, p2_r, la_s, la_r, gc_s, gc_r,
     gx_s, gx_r, rc_s, rc_r, rz_s, rz_r, rx_s, rx_r, ra_s, ra_r, rf_s, rf_r, rm_s, rm_r,
-    cy_s, cy_r, cz_s, cz_r, cc_s, cc_r,
+    cy_s, cy_r, cz_s, cz_r,
 ):
     z, fs, y = lax.axis_index("replica"), lax.axis_index("fsdp"), lax.axis_index("tensor")
     x, c = fs // 2, lax.rem(fs, 2)
@@ -105,14 +107,22 @@
     for k in RING_X:
         pl.semaphore_signal(barrier, inc=1, device_id=at_x(k), device_id_type=MESH)
     pl.semaphore_signal(barrier, inc=1, device_id=mate, device_id_type=MESH)
-    load_m = pltpu.make_async_copy(m_hbm, m.at[:, pl.ds(0, COLS)], m_sem)
-    load_m.start()
     load_q = pltpu.make_async_copy(q_hbm, q, q_sem)
     load_q.start()
+    block = ROWS // LOADS
+    loads = []
+    for k in range(LOADS):
+        rows = pl.ds(k * block, block)
+        loads.append(pltpu.make_async_copy(m_hbm.at[rows], m.at[rows, pl.ds(0, COLS)], m_sem.at[k]))
+        loads[k].start()
     m[:, COLS:PAD] = jnp.zeros((ROWS, PAD - COLS), bf16)
     load_q.wait()
-    load_m.wait()
-    ls[0] = jnp.dot(m[:, 0:COLS], q[...], preferred_element_type=f32).astype(bf16)
+    for k in range(LOADS):
+        rows = slice(k * block, (k + 1) * block)
+        loads[k].wait()
+        ls[0, rows, :] = jnp.dot(
+            m[rows, 0:COLS], q[...], preferred_element_type=f32
+        ).astype(bf16)
     pl.semaphore_wait(barrier, NY + NZ + NX - 2)
 
     def chunk(j):
@@ -184,12 +194,10 @@
         total = cz[it, 0]
         for s in range(1, NZ):
             total = total + cz[it, s]
-        cc[it, 0] = total
-        start(copy(cc.at[it, 0], cc.at[it, 1], cc_s, cc_r.at[it], mate))
+        column_sq[it] = total
 
     def column_scale(it):
-        copy(cc.at[it, 0], cc.at[it, 1], cc_s, cc_r.at[it], mate).wait_recv()
-        return math.sqrt(FF) / jnp.sqrt(cc[it, 0] + cc[it, 1] + norm_eps)
+        return math.sqrt(FF) / jnp.sqrt(column_sq[it] + norm_eps)
 
     def factorise(it):
         for k in RING_X:
@@ -216,68 +224,120 @@
             rx[it, 2].astype(f32) + rx[it, 3].astype(f32)
         )
 
-    def left_factor(it):
-        if it > 0:
-            there = ra.at[it - 1, 1 - c]
-            copy(there, there, ra_s, ra_r.at[it - 1], mate).wait_recv()
-            rows = ra[it - 1].reshape(CZ, R)
-            if it == 1:
-                ring_end()
-            ls[it] = jnp.dot(
-                ms[...], jnp.concatenate([rows, rows], 0), preferred_element_type=f32
-            ).astype(bf16)
+    def right_raw(it):
+        return ra[it].reshape(CZ, R)
+
+    def left_factor():
         for k in RING:
             t = lax.rem(y + k, NY)
-            start(copy(ls.at[it, pl.ds(t * LY, LY)], ly.at[it, y], ly_s.at[k], ly_r.at[it, y], at_y(k)))
-        if it > 0:
-            factorise(it - 1)
-            squares(it - 1, triangular(right_total(it - 1)) * (1.0 / NZ))
-        ring_at(it, "A")
-        total = ls[it, pl.ds(y * LY, LY), :].astype(f32)
+            start(copy(ls.at[0, pl.ds(t * LY, LY)], ly.at[y], ly_s.at[k], ly_r.at[y], at_y(k)))
+        ring_at(0, "A")
+        total = ls[0, pl.ds(y * LY, LY), :].astype(f32)
         for k in RING:
             s = lax.rem(y + k, NY)
-            copy(ly.at[it, s], ly.at[it, s], ly_s.at[k], ly_r.at[it, s], at_y(k)).wait_recv()
-            total = total + ly[it, s].astype(f32)
-        lz[it, z] = total.astype(bf16)
-        for k in RING:
-            start(copy(lz.at[it, z], lz.at[it, z], lz_s.at[k], lz_r.at[it, z], at_z(k)))
-        if it > 0:
-            squares_over_y(it - 1)
-        ring_at(it, "B")
+            copy(ly.at[s], ly.at[s], ly_s.at[k], ly_r.at[s], at_y(k)).wait_recv()
+            total = total + ly[s].astype(f32)
+        lz[z] = total.astype(bf16)
+        for k in RING:
+            start(copy(lz.at[z], lz.at[z], lz_s.at[k], lz_r.at[z], at_z(k)))
+        ring_at(0, "B")
         for k in RING:
             s = lax.rem(z + k, NZ)
-            copy(lz.at[it, s], lz.at[it, s], lz_s.at[k], lz_r.at[it, s], at_z(k)).wait_recv()
-        total = lz[it, 0].astype(f32)
+            copy(lz.at[s], lz.at[s], lz_s.at[k], lz_r.at[s], at_z(k)).wait_recv()
+        total = lz[0].astype(f32)
         for s in range(1, NZ):
-            total = total + lz[it, s].astype(f32)
-        total = total * (1.0 / NZ) if it == 0 else triangular(total) * (1.0 / NZ**2)
-        la[it, pl.ds(y * LY, LY), :] = total.astype(bf16)
-        mine = la.at[it, pl.ds(y * LY, LY)]
-        for k in RING:
-            start(copy(mine, mine, la_s.at[k], la_r.at[it, y], at_y(k)))
-        if it > 0:
-            squares_over_z(it - 1)
-        ring_at(it, "C")
+            total = total + lz[s].astype(f32)
+        la[0, pl.ds(y * LY, LY), :] = (total * (1.0 / NZ)).astype(bf16)
+        mine = la.at[0, pl.ds(y * LY, LY)]
+        for k in RING:
+            start(copy(mine, mine, la_s.at[0, k], la_r.at[0, 0, y], at_y(k)))
+        ring_at(0, "C")
         for k in RING:
             s = lax.rem(y + k, NY)
-            theirs = la.at[it, pl.ds(s * LY, LY)]
-            copy(theirs, theirs, la_s.at[k], la_r.at[it, s], at_y(k)).wait_recv()
+            theirs = la.at[0, pl.ds(s * LY, LY)]
+            copy(theirs, theirs, la_s.at[0, k], la_r.at[0, 0, s], at_y(k)).wait_recv()
+
+    def left_halves(it):
+        there = ra.at[it - 1, 1 - c]
+        copy(there, there, ra_s, ra_r.at[it - 1], mate).wait_recv()
+        rows = right_raw(it - 1)
+        if it == 1:
+            ring_end()
+        ls[it] = jnp.dot(
+            ms[...], jnp.concatenate([rows, rows], 0), preferred_element_type=f32
+        ).astype(bf16)
+
+        def ours(half, k):
+            return pl.ds(lax.rem((z if half else y) + k, NZ) * LS + half * (ROWS // 2), LS)
+
+        def other(half, k):
+            return at_z(k) if half else at_y(k)
+
+        me = (y, z)
+        for k in RING:
+            for half in range(2):
+                start(copy(ls.at[it, ours(half, k)], p1.at[it, half, me[half]],
+                           p1_s.at[half, k], p1_r.at[it, half, me[half]], other(half, k)))
+        factorise(it - 1)
+        squares(it - 1, triangular(right_raw(it - 1).astype(f32)) * (1.0 / NZ))
+        totals = [ls[it, ours(half, 0), :].astype(f32) for half in range(2)]
+        for k in RING:
+            for half in range(2):
+                s = lax.rem(me[half] + k, NZ)
+                there = p1.at[it, half, s]
+                copy(there, there, p1_s.at[half, k], p1_r.at[it, half, s], other(half, k)).wait_recv()
+                totals[half] = totals[half] + p1[it, half, s].astype(f32)
+        for half in range(2):
+            p2[it, half, me[1 - half]] = totals[half].astype(bf16)
+        for k in RING:
+            for half in range(2):
+                mine = p2.at[it, half, me[1 - half]]
+                start(copy(mine, mine, p2_s.at[half, k], p2_r.at[it, half, me[1 - half]],
+                           other(1 - half, k)))
+        squares_over_y(it - 1)
+        for k in RING:
+            for half in range(2):
+                s = lax.rem(me[1 - half] + k, NZ)
+                there = p2.at[it, half, s]
+                copy(there, there, p2_s.at[half, k], p2_r.at[it, half, s], other(1 - half, k)).wait_recv()
+        totals = []
+        for half in range(2):
+            total = p2[it, half, 0].astype(f32)
+            for s in range(1, NZ):
+                total = total + p2[it, half, s].astype(f32)
+            totals.append(total)
+        total = triangular(jnp.concatenate(totals, 0)) * (1.0 / NZ**2)
+        for half in range(2):
+            la[it, ours(half, 0), :] = total[half * LS : (half + 1) * LS, :].astype(bf16)
+        for k in RING:
+            for half in range(2):
+                mine = la.at[it, ours(half, 0)]
+                start(copy(mine, mine, la_s.at[half, k], la_r.at[it, half, me[half]], other(half, k)))
+        squares_over_z(it - 1)
+        for k in RING:
+            for half in range(2):
+                theirs = la.at[it, ours(half, k)]
+                s = lax.rem(me[half] + k, NZ)
+                copy(theirs, theirs, la_s.at[half, k], la_r.at[it, half, s], other(half, k)).wait_recv()
 
     def ring_at(it, point):
         if it == 0 and point in PLACES:
             ring_step(PLACES.index(point) + 1)
+
+    def product(left, k, half):
+        columns = pl.ds(pl.multiple_of(k * CZ + half * HALF, HALF), HALF)
+        return lax.dot_general(
+            m[:, columns], left, (((0,), (0,)), ((), ())), preferred_element_type=f32
+        )
 
     def right_factor(it):
         left = la[it]
         gs[it] = lax.dot_general(left, left, (((0,), (0,)), ((), ())), preferred_element_type=f32)
         start(copy(gs.at[it], gc.at[it], gc_s, gc_r.at[it], mate))
         if it == 0:
-            rcs[...] = (
-                lax.dot_general(m[...], left, (((0,), (0,)), ((), ())), preferred_element_type=f32)
-                .astype(bf16)
-                .reshape(NZ, 2, HALF, R)
-            )
-            to_mate = copy(rcs.at[:, 1 - c], rc, rc_s, rc_r.at[it], mate)
+            for k in range(NZ):
+                rcs[k] = product(left, k, 1 - c).astype(bf16)
+            to_mate = copy(rcs, rc, rc_s, rc_r.at[it], mate)
         else:
             both = lax.dot_general(ms[...], left, (((0,), (0,)), ((), ())), preferred_element_type=f32)
             both = (both[0:CZ, :] + both[CZ : 2 * CZ, :]).reshape(2, HALF, R)
@@ -285,13 +345,16 @@
             r2s[it] = both.astype(bf16)
             to_mate = copy(r2s.at[it, 1 - c], r2c.at[it], rc_s, rc_r.at[it], mate)
         start(to_mate)
+        if it == 0:
+            for k in range(NZ):
+                ro[k] = product(left, k, c)
         copy(gs.at[it], gc.at[it], gc_s, gc_r.at[it], mate).wait_recv()
         gx[it, x] = (gs[it] + gc[it]).astype(bf16)
         for k in RING_X:
             start(copy(gx.at[it, x], gx.at[it, x], gx_s.at[k], gx_r.at[it, x], at_x(k)))
         to_mate.wait_recv()
         if it == 0:
-            rzs[...] = (rcs[:, c].astype(f32) + rc[...].astype(f32)).astype(bf16)
+            rzs[...] = (ro[...] + rc[...].astype(f32)).astype(bf16)
             for k in RING:
                 t = lax.rem(z + k, NZ)
                 start(copy(rzs.at[t], rz.at[z], rz_s.at[k], rz_r.at[z], at_z(k)))
@@ -307,24 +370,29 @@
         for k in RING_X:
             start(copy(rx.at[it, x], rx.at[it, x], rx_s.at[k], rx_r.at[it, x], at_x(k)))
         ring_at(it, "E")
-        if it == ITERS - 1:
-            factorise(it)
         for k in RING_X:
             s = lax.rem(x + k, NX)
             copy(rx.at[it, s], rx.at[it, s], rx_s.at[k], rx_r.at[it, s], at_x(k)).wait_recv()
 
     last = ITERS - 1
     for it in range(ITERS):
-        left_factor(it)
+        if it == 0:
+            left_factor()
+        else:
+            left_halves(it)
         right_factor(it)
-        if it < last:
-            wait_sends()
-            ra[it, c] = right_total(it).astype(bf16)
-            start(copy(ra.at[it, c], ra.at[it, c], ra_s, ra_r.at[it], mate))
-
-    right = triangular(right_total(last)) * (1.0 / NZ)
+        ra[it, c] = right_total(it).astype(bf16)
+        to_mate = copy(ra.at[it, c], ra.at[it, c], ra_s, ra_r.at[it], mate)
+        to_mate.start()
+        wait_sends()
+        sends.append(to_mate)
+
+    factorise(last)
+    there = ra.at[last, 1 - c]
+    copy(there, there, ra_s, ra_r.at[last], mate).wait_recv()
+    right = triangular(right_raw(last).astype(f32)) * (1.0 / NZ)
     squares(last, right)
-    rf[z, c] = right.astype(bf16)
+    rf[z] = right.astype(bf16).reshape(2, HALF, R)
     mine = rf.at[z, c]
     for k in RING:
         start(copy(mine, mine, rf_s.at[k], rf_r.at[z], at_z(k)))
@@ -334,12 +402,12 @@
         s = lax.rem(z + k, NZ)
         there = rf.at[s, c]
         copy(there, there, rf_s.at[k], rf_r.at[s], at_z(k)).wait_recv()
-    half = rf.at[:, c]
-    start(copy(half, half, rm_s, rm_r, mate))
+    start(copy(rf.at[:, c], rfm, rm_s, rm_r, mate))
     squares_over_z(last)
-    half = rf.at[:, 1 - c]
-    copy(half, half, rm_s, rm_r, mate).wait_recv()
-    rr_ref[...] = rf[...].reshape(PAD, R)[0:COLS, :]
+    copy(rfm, rfm, rm_s, rm_r, mate).wait_recv()
+    for k in range(COLS // CZ):
+        rr_ref[pl.ds(k * CZ + c * HALF, HALF), :] = rf[k, c]
+        rr_ref[pl.ds(k * CZ + (1 - c) * HALF, HALF), :] = rfm[k]
     d_ref[...] = column_scale(last)
     wait_sends()
     for way in range(2):
@@ -367,15 +435,18 @@
             pltpu.VMEM((ROWS, 2 * CZ), bf16),
             pltpu.VMEM((2, 4, ROWS, CZ), bf16),
             pltpu.VMEM((n, ROWS, R), bf16),
-            pltpu.VMEM((n, NY, LY, R), bf16),
-            pltpu.VMEM((n, NZ, LY, R), bf16),
+            pltpu.VMEM((NY, LY, R), bf16),
+            pltpu.VMEM((NZ, LY, R), bf16),
+            pltpu.VMEM((n, 2, NY, LS, R), bf16),
+            pltpu.VMEM((n, 2, NZ, LS, R), bf16),
             pltpu.VMEM((n, ROWS, R), bf16),
             pltpu.VMEM((n, R, R), f32),
             pltpu.VMEM((n, NX, R, R), bf16),
             pltpu.VMEM((n, R, R), f32),
             pltpu.VMEM((R, 2 * R), f32),
-            pltpu.VMEM((NZ, 2, HALF, R), bf16),
             pltpu.VMEM((NZ, HALF, R), bf16),
+            pltpu.VMEM((NZ, HALF, R), bf16),
+            pltpu.VMEM((NZ, HALF, R), f32),
             pltpu.VMEM((NZ, HALF, R), bf16),
             pltpu.VMEM((NZ, HALF, R), bf16),
             pltpu.VMEM((2, HALF, R), f32),
@@ -384,14 +455,17 @@
             pltpu.VMEM((n, NX, HALF, R), bf16),
             pltpu.VMEM((n, 2, HALF, R), bf16),
             pltpu.VMEM((NZ, 2, HALF, R), bf16),
+            pltpu.VMEM((NZ, HALF, R), bf16),
             pltpu.VMEM((n, NY, 8, R), f32),
             pltpu.VMEM((n, NZ, 8, R), f32),
-            pltpu.VMEM((n, 2, 8, R), f32),
-            dma(()), dma(()),
+            pltpu.VMEM((n, 8, R), f32),
+            dma((LOADS,)), dma(()),
             dma((2, 4)), dma((2, 4)),
-            dma((NY,)), dma((n, NY)),
-            dma((NZ,)), dma((n, NZ)),
-            dma((NY,)), dma((n, NY)),
+            dma((NY,)), dma((NY,)),
+            dma((NZ,)), dma((NZ,)),
+            dma((2, NY)), dma((n, 2, NY)),
+            dma((2, NZ)), dma((n, 2, NZ)),
+            dma((2, NY)), dma((n, 2, NY)),
             dma(()), dma((n,)),
             dma((NX,)), dma((n, NX)),
             dma(()), dma((n,)),
@@ -402,7 +476,6 @@
             dma(()), dma(()),
             dma((NY,)), dma((n, NY)),
             dma((NZ,)), dma((n, NZ)),
-            dma(()), dma((n,)),
         ],
         compiler_params=pltpu.CompilerParams(
             collective_id=0, has_side_effects=True, vmem_limit_bytes=56 << 20

time: 119 us -> 117 us (0.983)
  Pallas kernels: 118 us -> 116 us
    pallas_call x1, Pallas kernels: 114 us -> 112 us  [iterate(): pl.pallas_call(iterate_kernel, out_shape=[jax.ShapeDtypeStruct((ROWS, R),...]
where the time goes in v7:
time: 117 us; the launch traced here: 116 us
  Pallas kernels  116 us (99%)
    pallas_call x1, Pallas kernels, iterate(): pl.pallas_call(iterate_kernel, out_shape=[jax.ShapeDtypeStruct((ROWS, R),...  112 us
    pallas_call x1, Pallas kernels, finish(): pl.pallas_call(finish_kernel, grid=(steps,), out_shape=[jax.ShapeDtypeStr...  3.38 us

profile of v7, /device:TPU:1, one launch (start us, length us, event | category | flops | bytes accessed | tf_op | source)
XLA Modules:
  0.0 116.4 jit_solution(16839235161258567535)
XLA Ops:
  0.6 112.4 %shard_map.49 = (bf16[512,128]{1,0:T(8,128)(2,1)}, bf16[1792,128]{1,0:T(8,128)(2,1)}, f32[8,128]{1,0:T(8,128)}) custom-call(bf16[512,1792]{1,0:T(8,128)(2,1)} %bitcast.2, bf16[1792,128]{1,0:T(8,128)(2,1)} %q_hbm.1), custom_call_target="tpu_custom_call" | custom-call | flops 1409286144 | bytes 1835008 | tf_op jit(solution)/shard_map/pallas_call | solution.py:423
  113.0 3.4 %shard_map.50 = (bf16[512,1792]{1,0:T(8,128)(2,1)}, f32[512,128]{1,0:T(8,128)}, bf16[1792,128]{1,0:T(8,128)(2,1)}) custom-call(bf16[512,1792]{1,0:T(8,128)(2,1)} %bitcast.3, bf16[512,128]{1,0:T(8,128)(2,1)} %get-tuple-element.9.left, bf16[1792,128]{1,0:T(8,128)(2,1)} %get-tuple-element.10.right, f32[8,128]{1,0:T(8,128)} %get-tuple-element.11.scale), custom_call_target="tpu_custom_call" | custom-call | flops 234881024 | bytes 3670016 | tf_op jit(solution)/shard_map/pallas_call | solution.py:504

commit v8 on v7

--- a/solution.py
+++ b/solution.py
@@ -20,10 +20,11 @@
 CZ = 2 * HALF
 PAD = NZ * CZ
 LS = LY // 2
-LOADS = 4
+HR = ROWS // 2
 LINKS = (4, 3)
 RING = (4, 3, 5, 2, 6, 1, 7)
 RING_X = (2, 1, 3)
+NEAR, NEAR_X = RING[::-1], RING_X[::-1]
 PLACES = "ABCD"
 
 ridge_scale = 1e-06
@@ -109,20 +110,12 @@
     pl.semaphore_signal(barrier, inc=1, device_id=mate, device_id_type=MESH)
     load_q = pltpu.make_async_copy(q_hbm, q, q_sem)
     load_q.start()
-    block = ROWS // LOADS
-    loads = []
-    for k in range(LOADS):
-        rows = pl.ds(k * block, block)
-        loads.append(pltpu.make_async_copy(m_hbm.at[rows], m.at[rows, pl.ds(0, COLS)], m_sem.at[k]))
-        loads[k].start()
+    load_m = pltpu.make_async_copy(m_hbm, m.at[:, pl.ds(0, COLS)], m_sem)
+    load_m.start()
     m[:, COLS:PAD] = jnp.zeros((ROWS, PAD - COLS), bf16)
     load_q.wait()
-    for k in range(LOADS):
-        rows = slice(k * block, (k + 1) * block)
-        loads[k].wait()
-        ls[0, rows, :] = jnp.dot(
-            m[rows, 0:COLS], q[...], preferred_element_type=f32
-        ).astype(bf16)
+    load_m.wait()
+    ls[0] = jnp.dot(m[:, 0:COLS], q[...], preferred_element_type=f32).astype(bf16)
     pl.semaphore_wait(barrier, NY + NZ + NX - 2)
 
     def chunk(j):
@@ -131,28 +124,33 @@
     def ring_chunk(way, step):
         return chunk(z + 5 - step if way == 0 else z - 4 + step)
 
-    def ring_copy(way, step):
-        src = m.at[:, ring_chunk(way, 1)] if step == 1 else ring.at[way, step - 2]
-        return copy(src, ring.at[way, step - 1], ring_s.at[way, step - 1],
-                    ring_r.at[way, step - 1], at_z(1 if way == 0 else NZ - 1))
+    def ring_copy(way, half, step):
+        rows = pl.ds(half * HR, HR)
+        src = m.at[rows, ring_chunk(way, 1)] if step == 1 else ring.at[way, half, step - 2]
+        return copy(src, ring.at[way, half, step - 1], ring_s.at[way, half, step - 1],
+                    ring_r.at[way, half, step - 1], at_z(1 if way == 0 else NZ - 1))
 
     def ring_step(step):
-        for way in range(2):
-            if step <= LINKS[way]:
-                if step > 1:
-                    ring_copy(way, step - 1).wait_recv()
-                    own = m[:, ring_chunk(way, step)].astype(f32)
-                    ring[way, step - 2] = (ring[way, step - 2].astype(f32) + own).astype(bf16)
-                ring_copy(way, step).start()
+        for half in range(2):
+            for way in range(2):
+                if step <= LINKS[way]:
+                    if step > 1:
+                        ring_copy(way, half, step - 1).wait_recv()
+                        own = m[pl.ds(half * HR, HR), ring_chunk(way, step)].astype(f32)
+                        come = ring[way, half, step - 2].astype(f32)
+                        ring[way, half, step - 2] = (come + own).astype(bf16)
+                    ring_copy(way, half, step).start()
 
     def ring_end():
-        total = m[:, chunk(z)].astype(f32)
-        for way in range(2):
-            ring_copy(way, LINKS[way]).wait_recv()
-            total = total + ring[way, LINKS[way] - 1].astype(f32)
-        high = total.astype(bf16)
-        ms[:, 0:CZ] = high
-        ms[:, CZ : 2 * CZ] = (total - high.astype(f32)).astype(bf16)
+        for half in range(2):
+            rows = slice(half * HR, (half + 1) * HR)
+            total = m[rows, chunk(z)].astype(f32)
+            for way in range(2):
+                ring_copy(way, half, LINKS[way]).wait_recv()
+                total = total + ring[way, half, LINKS[way] - 1].astype(f32)
+            high = total.astype(bf16)
+            ms[rows, 0:CZ] = high
+            ms[rows, CZ : 2 * CZ] = (total - high.astype(f32)).astype(bf16)
 
     sends = []
 
@@ -177,7 +175,7 @@
             start(copy(cy.at[it, y], cy.at[it, y], cy_s.at[k], cy_r.at[it, y], at_y(k)))
 
     def squares_over_y(it):
-        for k in RING:
+        for k in NEAR:
             s = lax.rem(y + k, NY)
             copy(cy.at[it, s], cy.at[it, s], cy_s.at[k], cy_r.at[it, s], at_y(k)).wait_recv()
         total = cy[it, 0]
@@ -188,7 +186,7 @@
             start(copy(cz.at[it, z], cz.at[it, z], cz_s.at[k], cz_r.at[it, z], at_z(k)))
 
     def squares_over_z(it):
-        for k in RING:
+        for k in NEAR:
             s = lax.rem(z + k, NZ)
             copy(cz.at[it, s], cz.at[it, s], cz_s.at[k], cz_r.at[it, s], at_z(k)).wait_recv()
         total = cz[it, 0]
@@ -200,7 +198,7 @@
         return math.sqrt(FF) / jnp.sqrt(column_sq[it] + norm_eps)
 
     def factorise(it):
-        for k in RING_X:
+        for k in NEAR_X:
             s = lax.rem(x + k, NX)
             copy(gx.at[it, s], gx.at[it, s], gx_s.at[k], gx_r.at[it, s], at_x(k)).wait_recv()
         gram = (gx[it, 0].astype(f32) + gx[it, 1].astype(f32)) + (
@@ -233,7 +231,7 @@
             start(copy(ls.at[0, pl.ds(t * LY, LY)], ly.at[y], ly_s.at[k], ly_r.at[y], at_y(k)))
         ring_at(0, "A")
         total = ls[0, pl.ds(y * LY, LY), :].astype(f32)
-        for k in RING:
+        for k in NEAR:
             s = lax.rem(y + k, NY)
             copy(ly.at[s], ly.at[s], ly_s.at[k], ly_r.at[s], at_y(k)).wait_recv()
             total = total + ly[s].astype(f32)
@@ -241,7 +239,7 @@
         for k in RING:
             start(copy(lz.at[z], lz.at[z], lz_s.at[k], lz_r.at[z], at_z(k)))
         ring_at(0, "B")
-        for k in RING:
+        for k in NEAR:
             s = lax.rem(z + k, NZ)
             copy(lz.at[s], lz.at[s], lz_s.at[k], lz_r.at[s], at_z(k)).wait_recv()
         total = lz[0].astype(f32)
@@ -252,7 +250,7 @@
         for k in RING:
             start(copy(mine, mine, la_s.at[0, k], la_r.at[0, 0, y], at_y(k)))
         ring_at(0, "C")
-        for k in RING:
+        for k in NEAR:
             s = lax.rem(y + k, NY)
             theirs = la.at[0, pl.ds(s * LY, LY)]
             copy(theirs, theirs, la_s.at[0, k], la_r.at[0, 0, s], at_y(k)).wait_recv()
@@ -261,8 +259,6 @@
         there = ra.at[it - 1, 1 - c]
         copy(there, there, ra_s, ra_r.at[it - 1], mate).wait_recv()
         rows = right_raw(it - 1)
-        if it == 1:
-            ring_end()
         ls[it] = jnp.dot(
             ms[...], jnp.concatenate([rows, rows], 0), preferred_element_type=f32
         ).astype(bf16)
@@ -281,7 +277,7 @@
         factorise(it - 1)
         squares(it - 1, triangular(right_raw(it - 1).astype(f32)) * (1.0 / NZ))
         totals = [ls[it, ours(half, 0), :].astype(f32) for half in range(2)]
-        for k in RING:
+        for k in NEAR:
             for half in range(2):
                 s = lax.rem(me[half] + k, NZ)
                 there = p1.at[it, half, s]
@@ -295,7 +291,7 @@
                 start(copy(mine, mine, p2_s.at[half, k], p2_r.at[it, half, me[1 - half]],
                            other(1 - half, k)))
         squares_over_y(it - 1)
-        for k in RING:
+        for k in NEAR:
             for half in range(2):
                 s = lax.rem(me[1 - half] + k, NZ)
                 there = p2.at[it, half, s]
@@ -314,7 +310,7 @@
                 mine = la.at[it, ours(half, 0)]
                 start(copy(mine, mine, la_s.at[half, k], la_r.at[it, half, me[half]], other(half, k)))
         squares_over_z(it - 1)
-        for k in RING:
+        for k in NEAR:
             for half in range(2):
                 theirs = la.at[it, ours(half, k)]
                 s = lax.rem(me[half] + k, NZ)
@@ -323,20 +319,17 @@
     def ring_at(it, point):
         if it == 0 and point in PLACES:
             ring_step(PLACES.index(point) + 1)
-
-    def product(left, k, half):
-        columns = pl.ds(pl.multiple_of(k * CZ + half * HALF, HALF), HALF)
-        return lax.dot_general(
-            m[:, columns], left, (((0,), (0,)), ((), ())), preferred_element_type=f32
-        )
 
     def right_factor(it):
         left = la[it]
         gs[it] = lax.dot_general(left, left, (((0,), (0,)), ((), ())), preferred_element_type=f32)
         start(copy(gs.at[it], gc.at[it], gc_s, gc_r.at[it], mate))
         if it == 0:
-            for k in range(NZ):
-                rcs[k] = product(left, k, 1 - c).astype(bf16)
+            ro[...] = (
+                lax.dot_general(m[...], left, (((0,), (0,)), ((), ())), preferred_element_type=f32)
+                .reshape(NZ, 2, HALF, R)
+            )
+            rcs[...] = ro[:, 1 - c].astype(bf16)
             to_mate = copy(rcs, rc, rc_s, rc_r.at[it], mate)
         else:
             both = lax.dot_general(ms[...], left, (((0,), (0,)), ((), ())), preferred_element_type=f32)
@@ -345,22 +338,19 @@
             r2s[it] = both.astype(bf16)
             to_mate = copy(r2s.at[it, 1 - c], r2c.at[it], rc_s, rc_r.at[it], mate)
         start(to_mate)
-        if it == 0:
-            for k in range(NZ):
-                ro[k] = product(left, k, c)
         copy(gs.at[it], gc.at[it], gc_s, gc_r.at[it], mate).wait_recv()
         gx[it, x] = (gs[it] + gc[it]).astype(bf16)
         for k in RING_X:
             start(copy(gx.at[it, x], gx.at[it, x], gx_s.at[k], gx_r.at[it, x], at_x(k)))
         to_mate.wait_recv()
         if it == 0:
-            rzs[...] = (ro[...] + rc[...].astype(f32)).astype(bf16)
+            rzs[...] = (ro[:, c] + rc[...].astype(f32)).astype(bf16)
             for k in RING:
                 t = lax.rem(z + k, NZ)
                 start(copy(rzs.at[t], rz.at[z], rz_s.at[k], rz_r.at[z], at_z(k)))
             ring_at(it, "D")
             total = rzs[z].astype(f32)
-            for k in RING:
+            for k in NEAR:
                 s = lax.rem(z + k, NZ)
                 copy(rz.at[s], rz.at[s], rz_s.at[k], rz_r.at[s], at_z(k)).wait_recv()
                 total = total + rz[s].astype(f32)
@@ -370,7 +360,7 @@
         for k in RING_X:
             start(copy(rx.at[it, x], rx.at[it, x], rx_s.at[k], rx_r.at[it, x], at_x(k)))
         ring_at(it, "E")
-        for k in RING_X:
+        for k in NEAR_X:
             s = lax.rem(x + k, NX)
             copy(rx.at[it, s], rx.at[it, s], rx_s.at[k], rx_r.at[it, s], at_x(k)).wait_recv()
 
@@ -384,6 +374,8 @@
         ra[it, c] = right_total(it).astype(bf16)
         to_mate = copy(ra.at[it, c], ra.at[it, c], ra_s, ra_r.at[it], mate)
         to_mate.start()
+        if it == 0:
+            ring_end()
         wait_sends()
         sends.append(to_mate)
 
@@ -398,7 +390,7 @@
         start(copy(mine, mine, rf_s.at[k], rf_r.at[z], at_z(k)))
     lr_ref[...] = triangular(la[last].astype(f32)).astype(bf16)
     squares_over_y(last)
-    for k in RING:
+    for k in NEAR:
         s = lax.rem(z + k, NZ)
         there = rf.at[s, c]
         copy(there, there, rf_s.at[k], rf_r.at[s], at_z(k)).wait_recv()
@@ -411,8 +403,9 @@
     d_ref[...] = column_scale(last)
     wait_sends()
     for way in range(2):
-        for step in range(1, LINKS[way] + 1):
-            ring_copy(way, step).wait_send()
+        for half in range(2):
+            for step in range(1, LINKS[way] + 1):
+                ring_copy(way, half, step).wait_send()
 
 
 def iterate(block, q):
@@ -433,7 +426,7 @@
             pltpu.VMEM((ROWS, PAD), bf16),
             pltpu.VMEM((COLS, R), bf16),
             pltpu.VMEM((ROWS, 2 * CZ), bf16),
-            pltpu.VMEM((2, 4, ROWS, CZ), bf16),
+            pltpu.VMEM((2, 2, 4, HR, CZ), bf16),
             pltpu.VMEM((n, ROWS, R), bf16),
             pltpu.VMEM((NY, LY, R), bf16),
             pltpu.VMEM((NZ, LY, R), bf16),
@@ -446,7 +439,7 @@
             pltpu.VMEM((R, 2 * R), f32),
             pltpu.VMEM((NZ, HALF, R), bf16),
             pltpu.VMEM((NZ, HALF, R), bf16),
-            pltpu.VMEM((NZ, HALF, R), f32),
+            pltpu.VMEM((NZ, 2, HALF, R), f32),
             pltpu.VMEM((NZ, HALF, R), bf16),
             pltpu.VMEM((NZ, HALF, R), bf16),
             pltpu.VMEM((2, HALF, R), f32),
@@ -459,8 +452,8 @@
             pltpu.VMEM((n, NY, 8, R), f32),
             pltpu.VMEM((n, NZ, 8, R), f32),
             pltpu.VMEM((n, 8, R), f32),
-            dma((LOADS,)), dma(()),
-            dma((2, 4)), dma((2, 4)),
+            dma(()), dma(()),
+            dma((2, 2, 4)), dma((2, 2, 4)),
             dma((NY,)), dma((NY,)),
             dma((NZ,)), dma((NZ,)),
             dma((2, NY)), dma((n, 2, NY)),

time: 117 us -> 115 us (0.983)
  Pallas kernels: 116 us -> 114 us
    pallas_call x1, Pallas kernels: 112 us -> 111 us  [iterate(): pl.pallas_call(iterate_kernel, out_shape=[jax.ShapeDtypeStruct((ROWS, R),...]
where the time goes in v8:
time: 115 us
  Pallas kernels  114 us (99%)
    pallas_call x1, Pallas kernels, iterate(): pl.pallas_call(iterate_kernel, out_shape=[jax.ShapeDtypeStruct((ROWS, R),...  111 us
    pallas_call x1, Pallas kernels, finish(): pl.pallas_call(finish_kernel, grid=(steps,), out_shape=[jax.ShapeDtypeStr...  3.38 us

profile of v8, /device:TPU:1, one launch (start us, length us, event | category | flops | bytes accessed | tf_op | source)
XLA Modules:
  0.0 114.9 jit_solution(14474942758896550962)
XLA Ops:
  0.6 110.9 %shard_map.49 = (bf16[512,128]{1,0:T(8,128)(2,1)}, bf16[1792,128]{1,0:T(8,128)(2,1)}, f32[8,128]{1,0:T(8,128)}) custom-call(bf16[512,1792]{1,0:T(8,128)(2,1)} %bitcast.2, bf16[1792,128]{1,0:T(8,128)(2,1)} %q_hbm.1), custom_call_target="tpu_custom_call" | custom-call | flops 1409286144 | bytes 1835008 | tf_op jit(solution)/shard_map/pallas_call | solution.py:416
  111.5 3.4 %shard_map.50 = (bf16[512,1792]{1,0:T(8,128)(2,1)}, f32[512,128]{1,0:T(8,128)}, bf16[1792,128]{1,0:T(8,128)(2,1)}) custom-call(bf16[512,1792]{1,0:T(8,128)(2,1)} %bitcast.3, bf16[512,128]{1,0:T(8,128)(2,1)} %get-tuple-element.9.left, bf16[1792,128]{1,0:T(8,128)(2,1)} %get-tuple-element.10.right, f32[8,128]{1,0:T(8,128)} %get-tuple-element.11.scale), custom_call_target="tpu_custom_call" | custom-call | flops 234881024 | bytes 3670016 | tf_op jit(solution)/shard_map/pallas_call | solution.py:497

commit v9 on v8

--- a/solution.py
+++ b/solution.py
@@ -198,6 +198,9 @@
         return math.sqrt(FF) / jnp.sqrt(column_sq[it] + norm_eps)
 
     def factorise(it):
+        if it > 0:
+            scale = jnp.broadcast_to(column_scale(it - 1)[0:1, :], (R, R))
+            scales = scale * scale.T
         for k in NEAR_X:
             s = lax.rem(x + k, NX)
             copy(gx.at[it, s], gx.at[it, s], gx_s.at[k], gx_r.at[it, s], at_x(k)).wait_recv()
@@ -205,8 +208,7 @@
             gx[it, 2].astype(f32) + gx[it, 3].astype(f32)
         )
         if it > 0:
-            scale = jnp.broadcast_to(column_scale(it - 1)[0:1, :], (R, R))
-            gram = gram * scale * scale.T
+            gram = gram * scales
         eye = lax.broadcasted_iota(jnp.int32, (R, R), 0) == lax.broadcasted_iota(
             jnp.int32, (R, R), 1
         )
@@ -325,24 +327,29 @@
         gs[it] = lax.dot_general(left, left, (((0,), (0,)), ((), ())), preferred_element_type=f32)
         start(copy(gs.at[it], gc.at[it], gc_s, gc_r.at[it], mate))
         if it == 0:
-            ro[...] = (
-                lax.dot_general(m[...], left, (((0,), (0,)), ((), ())), preferred_element_type=f32)
-                .reshape(NZ, 2, HALF, R)
-            )
-            rcs[...] = ro[:, 1 - c].astype(bf16)
-            to_mate = copy(rcs, rc, rc_s, rc_r.at[it], mate)
+            to_mate = []
+            for k in range(2):
+                chips, columns = slice(k * 4, k * 4 + 4), slice(k * 4 * CZ, (k * 4 + 4) * CZ)
+                ro[chips] = lax.dot_general(
+                    m[:, columns], left, (((0,), (0,)), ((), ())), preferred_element_type=f32
+                ).reshape(4, 2, HALF, R)
+                rcs[chips] = ro[chips, 1 - c].astype(bf16)
+                part = pl.ds(k * 4, 4)
+                to_mate.append(copy(rcs.at[part], rc.at[part], rc_s.at[k], rc_r.at[it, k], mate))
+                start(to_mate[k])
         else:
             both = lax.dot_general(ms[...], left, (((0,), (0,)), ((), ())), preferred_element_type=f32)
             both = (both[0:CZ, :] + both[CZ : 2 * CZ, :]).reshape(2, HALF, R)
             r2[...] = both
             r2s[it] = both.astype(bf16)
-            to_mate = copy(r2s.at[it, 1 - c], r2c.at[it], rc_s, rc_r.at[it], mate)
-        start(to_mate)
+            to_mate = [copy(r2s.at[it, 1 - c], r2c.at[it], rc_s.at[0], rc_r.at[it, 0], mate)]
+            start(to_mate[0])
         copy(gs.at[it], gc.at[it], gc_s, gc_r.at[it], mate).wait_recv()
         gx[it, x] = (gs[it] + gc[it]).astype(bf16)
         for k in RING_X:
             start(copy(gx.at[it, x], gx.at[it, x], gx_s.at[k], gx_r.at[it, x], at_x(k)))
-        to_mate.wait_recv()
+        for cp in to_mate:
+            cp.wait_recv()
         if it == 0:
             rzs[...] = (ro[:, c] + rc[...].astype(f32)).astype(bf16)
             for k in RING:
@@ -461,7 +468,7 @@
             dma((2, NY)), dma((n, 2, NY)),
             dma(()), dma((n,)),
             dma((NX,)), dma((n, NX)),
-            dma(()), dma((n,)),
+            dma((2,)), dma((n, 2)),
             dma((NZ,)), dma((NZ,)),
             dma((NX,)), dma((n, NX)),
             dma(()), dma((n,)),

time: 115 us -> 114 us (level)
  no operation moved by 1% of the time
where the time goes in v9:
time: 114 us
  Pallas kernels  114 us (100%)
    pallas_call x1, Pallas kernels, iterate(): pl.pallas_call(iterate_kernel, out_shape=[jax.ShapeDtypeStruct((ROWS, R),...  110 us
    pallas_call x1, Pallas kernels, finish(): pl.pallas_call(finish_kernel, grid=(steps,), out_shape=[jax.ShapeDtypeStr...  3.38 us

profile of v9, /device:TPU:1, one launch (start us, length us, event | category | flops | bytes accessed | tf_op | source)
XLA Modules:
  0.0 114.3 jit_solution(13322276090414480445)
XLA Ops:
  0.6 110.3 %shard_map.49 = (bf16[512,128]{1,0:T(8,128)(2,1)}, bf16[1792,128]{1,0:T(8,128)(2,1)}, f32[8,128]{1,0:T(8,128)}) custom-call(bf16[512,1792]{1,0:T(8,128)(2,1)} %bitcast.2, bf16[1792,128]{1,0:T(8,128)(2,1)} %q_hbm.1), custom_call_target="tpu_custom_call" | custom-call | flops 1409286144 | bytes 1835008 | tf_op jit(solution)/shard_map/pallas_call | solution.py:423
  110.9 3.4 %shard_map.50 = (bf16[512,1792]{1,0:T(8,128)(2,1)}, f32[512,128]{1,0:T(8,128)}, bf16[1792,128]{1,0:T(8,128)(2,1)}) custom-call(bf16[512,1792]{1,0:T(8,128)(2,1)} %bitcast.3, bf16[512,128]{1,0:T(8,128)(2,1)} %get-tuple-element.9.left, bf16[1792,128]{1,0:T(8,128)(2,1)} %get-tuple-element.10.right, f32[8,128]{1,0:T(8,128)} %get-tuple-element.11.scale), custom_call_target="tpu_custom_call" | custom-call | flops 234881024 | bytes 3670016 | tf_op jit(solution)/shard_map/pallas_call | solution.py:504
